TPU v7x, 512 devices: a whole 4x4x16 slice. The times are simulated.
512 devices in a mesh: dp: 16 (over z_hi, x, core), fsdp: 32 (over y, z_lo).
Axes of the slice: x: 4, y: 4, z: 16 (z_hi: 2, z_lo: 8; z = z_hi * 8 + z_lo), core: 2. Of those that a mesh axis runs over, the one named last changes fastest.
Arguments:
- tokens: bfloat16 [65536, 8192], P(('dp', 'fsdp')), may hold values from -6 to 6
- norm_gain: bfloat16 [8192], replicated, may hold values from 0.25 to 1.75
- value_weight: bfloat16 [8192, 512], P('fsdp'), may hold values from -0.0625 to 0.0625
- input_basis: bfloat16 [8192, 64], P('fsdp'), may hold values from -0.0625 to 0.0625
- output_basis: bfloat16 [512, 64], replicated, may hold values from -0.25 to 0.25
- rotated_queries: bfloat16 [65536, 4096], P(('dp', 'fsdp')), may hold values from -150 to 150
- rotated_keys: bfloat16 [65536, 512], P(('dp', 'fsdp')), may hold values from -6 to 6
- upstream_grad: bfloat16 [65536, 4096], P(('dp', 'fsdp')), may hold values from -6 to 6
- example_lengths: int32 [512, 8], P(('dp', 'fsdp')), may hold values from 1 to 64, 128 in all within a row
- query_grads: bfloat16 [1024, 4096], P(('dp', 'fsdp')), may hold values from -0.0234375 to 0.0234375
Outputs:
- key_grad: bfloat16 [65536, 512], P(('dp', 'fsdp'))
- influence: float32 [4096, 1024], P(('dp', 'fsdp'))
Inputs may be any that keep to these rules, and one draw needn't show every extreme that they name: `example_lengths`: each row sums to 128; its largest entry is 64.
All inputs are finite; a program needn't handle non-finite values.
Results may differ from a plain program's by a relative error of at most 0.014.
Values may be sent and summed in bfloat16 or wider, within the bound.
No kernel may reach another device: no remote copies, remote signals or barrier semaphores. Data moves between devices by JAX's collectives and lax.ppermute only.
A program may use at most 64 MiB of HBM per device.

v0:
```python
import math

import jax
import jax.numpy as jnp
from jax import lax
from jax.sharding import PartitionSpec as P

HD = 128
GROUP = 8
KVH = 4


epsilon = 1e-05


def shifted(block, axis, distance):
    devices = range(lax.axis_size(axis))
    route = [((i - distance) % len(devices), i) for i in devices]
    return lax.ppermute(block, axis, route)


def attend(queries, keys, values, upstream, lengths):
    count = queries.shape[0]
    query_heads = queries.reshape(count, KVH, GROUP, HD)
    key_heads = keys.reshape(count, KVH, HD)
    value_heads = values.reshape(count, KVH, HD)
    grad_heads = upstream.reshape(count, KVH, GROUP, HD)
    bounds = jnp.cumsum(lengths)
    places = jnp.arange(count, dtype=jnp.int32)
    segment = jnp.sum((places[:, None] >= bounds[None, :]).astype(jnp.int32), axis=1)
    allowed = (segment[:, None] == segment[None, :]) & (places[None, :] <= places[:, None])
    scale = 1.0 / math.sqrt(HD)
    logits = (
        jnp.einsum("tjgd,ujd->jgtu", query_heads, key_heads, preferred_element_type=jnp.float32)
        * scale
    )
    logits = jnp.where(allowed, logits, jnp.float32(-1e30))
    row_max = jnp.max(logits, axis=-1, keepdims=True)
    expo = jnp.exp(logits - row_max)
    probs = expo / jnp.sum(expo, axis=-1, keepdims=True)
    probs_low = probs.astype(jnp.bfloat16)
    value_grad = jnp.einsum(
        "jgtu,tjgd->ujd", probs_low, grad_heads, preferred_element_type=jnp.float32
    ).astype(jnp.bfloat16)
    prob_grad = jnp.einsum(
        "tjgd,ujd->jgtu", grad_heads, value_heads, preferred_element_type=jnp.float32
    )
    logit_grad = probs * (prob_grad - jnp.sum(probs * prob_grad, axis=-1, keepdims=True))
    logit_low = logit_grad.astype(jnp.bfloat16)
    key_grad = (
        jnp.einsum("jgtu,tjgd->ujd", logit_low, query_heads, preferred_element_type=jnp.float32)
        * scale
    ).astype(jnp.bfloat16)
    onehot = (segment[:, None] == jnp.arange(lengths.shape[0], dtype=jnp.int32)[None, :]).astype(
        jnp.float32
    )
    return (key_grad.reshape(count, KVH * HD), value_grad.reshape(count, KVH * HD), onehot)


def place_scores(train_grads, tally, holding, source):
    block_scores = lax.dot_general(
        train_grads, holding, (((1,), (1,)), ((), ())), preferred_element_type=jnp.float32
    )
    return lax.dynamic_update_slice_in_dim(tally, block_scores, source * holding.shape[0], 1)


def circulate_scores(train_grads, query_grads):
    cycle_len = lax.axis_size("dp")
    cycle_pos = lax.axis_index("dp")
    group_rows = query_grads.shape[0] * lax.axis_size("fsdp")
    start_block = lax.all_gather(query_grads, "fsdp", axis=0, tiled=True)

    def advance_ahead(holding):
        return shifted(holding, "dp", 1)

    tally = jnp.zeros((train_grads.shape[0], cycle_len * group_rows), jnp.float32)
    tally = place_scores(train_grads, tally, start_block, cycle_pos)

    def one_turn(turn_index, carry):
        holding, scores_now = carry
        holding = advance_ahead(holding)
        source = (cycle_pos - turn_index - 1) % cycle_len
        return (holding, place_scores(train_grads, scores_now, holding, source))

    final_block, tally = lax.fori_loop(0, cycle_len - 1, one_turn, (start_block, tally))
    return tally


def cycle_scores(train_grads, query_grads):
    return circulate_scores(train_grads, query_grads)


def on_device(
    tokens,
    norm_gain,
    value_weight,
    input_basis,
    output_basis,
    rotated_queries,
    rotated_keys,
    upstream_grad,
    example_lengths,
    query_grads,
):
    activ = tokens.astype(jnp.float32)
    mean_square = jnp.mean(activ * activ, axis=1, keepdims=True)
    normed = (activ * lax.rsqrt(mean_square + epsilon) * norm_gain.astype(jnp.float32)).astype(
        jnp.bfloat16
    )
    value_sum = jnp.dot(
        normed,
        lax.all_gather(value_weight, "fsdp", axis=0, tiled=True),
        preferred_element_type=jnp.float32,
    )
    left = jnp.dot(
        normed,
        lax.all_gather(input_basis, "fsdp", axis=0, tiled=True),
        preferred_element_type=jnp.float32,
    )
    values = value_sum.astype(jnp.bfloat16)
    key_grad, value_grad, onehot = attend(
        rotated_queries, rotated_keys, values, upstream_grad, example_lengths[0]
    )
    right = jnp.dot(value_grad, output_basis, preferred_element_type=jnp.float32)
    per_example = jnp.einsum("te,ti,tj->eij", onehot, left, right, precision=lax.Precision.HIGHEST)
    train_grads = per_example.reshape(onehot.shape[1], left.shape[1] * right.shape[1]).astype(
        jnp.bfloat16
    )
    influence = cycle_scores(train_grads, query_grads)
    return (key_grad, influence)


def solution(mesh):
    return jax.shard_map(
        on_device,
        mesh=mesh,
        in_specs=(
            P(("dp", "fsdp"), None),
            P(),
            P("fsdp", None),
            P("fsdp", None),
            P(),
            P(("dp", "fsdp"), None),
            P(("dp", "fsdp"), None),
            P(("dp", "fsdp"), None),
            P(("dp", "fsdp"), None),
            P(("dp", "fsdp"), None),
        ),
        out_specs=(P(("dp", "fsdp"), None), P(("dp", "fsdp"), None)),
        check_vma=False,
    )
```

profile of v0, /device:TPU:1, one launch (start us, length us, event | category | flops | bytes accessed | tf_op | source)
XLA Modules:
  0.0 859.8 jit_solution(7761603396690099430)
XLA Ops:
  11.2 117.9 %all-gather = bf16[32,2,4096]{2,1,0:T(2,128)(2,1)S(1)} all-gather(bf16[1,2,4096]{2,1,0:T(2,128)(2,1)} %bitcast.71), channel_id=1, replica_groups=mesh['dp'=16,'fsdp'=32] {'fsdp'}, dimensions={0}, use_global_device_ids=true | all-gather | bytes 540672 | tf_op jit(solution)/shard_map/all_gather | solution.py:71
  132.1 2.2 fusion.38
  134.3 2.5 fusion.10
  137.5 43.4 %all-gather.6.cloned.1.call-done = bf16[8192,64]{0,1:T(8,128)(2,1)} async-done(((bf16[256,64]{0,1:T(8,128)(2,1)}), bf16[8192,64]{0,1:T(8,128)(2,1)}) %all-gather.6.cloned.1.call-update) | async-done | bytes 1048592 | tf_op jit(solution)/shard_map/all_gather | solution.py:117
  180.8 2.1 fusion.18
  184.0 245.8 %all-gather.4.cloned.1.call-done = bf16[8192,512]{1,0:T(8,128)(2,1)} async-done(((bf16[256,512]{1,0:T(8,128)(2,1)}), bf16[8192,512]{1,0:T(8,128)(2,1)}) %all-gather.4.cloned.1.call-update) | async-done | bytes 8388624 | tf_op jit(solution)/shard_map/all_gather | solution.py:112
  429.8 4.7 convolution_convert_fusion.1
  434.5 2.5 fusion.4
  438.7 413.6 %while.17 = (s32[]{:T(128)}, bf16[64,4096]{1,0:T(8,128)(2,1)S(1)}, f32[8,1024]{1,0:T(8,128)S(1)}, bf16[8,4096]{1,0:T(8,128)(2,1)S(1)}, s32[]{:T(128)}, /*index=5...) while((s32[]{:T(128)}, bf16[64,4096]{1,0:T(8,128)(2,1)S(1)}, ...), condition=%wide.region_7.8_spmd, body=%wide.region_6.7_spmd.sunk | while | flops 4194323 | bytes 3742036 | solution.py:85
  438.7 22.4 %collective-permute-start = (bf16[64,4096]{1,0:T(8,128)(2,1)S(1)}, bf16[64,4096]{1,0:T(8,128)(2,1)S(1)}, u32[]{:S(2)}, u32[]{:S(2)}) collective-permute-start(bf16[64,4096]{1,0:T(8,128)(2,1)S(1)} %get-tuple-element.203), channel_id=1, source_target_pairs={{480,0},{0,32},{32,64},{64,96},{96,128},{128,160},{160,192},{192,2... | collective-permute-start | bytes 1572872 | tf_op jit(solution)/shard_map/while/body/eval_jaxpr/ppermute | solution.py:19
  461.2 6.1 collective-permute-done
  467.7 4.4 collective-permute-start
  472.2 18.4 %collective-permute-done = bf16[64,4096]{1,0:T(8,128)(2,1)S(1)} collective-permute-done((bf16[64,4096]{1,0:T(8,128)(2,1)S(1)}, bf16[64,4096]{1,0:T(8,128)(2,1)S(1)}, u32[]{:S(2)}, u32[]{:S(2)}) %collective-permute-start) | collective-permute-done | bytes 524320 | tf_op jit(solution)/shard_map/while/body/eval_jaxpr/ppermute | solution.py:19
  491.1 1.9 collective-permute-start
  493.0 29.4 %collective-permute-done = bf16[64,4096]{1,0:T(8,128)(2,1)S(1)} collective-permute-done((bf16[64,4096]{1,0:T(8,128)(2,1)S(1)}, bf16[64,4096]{1,0:T(8,128)(2,1)S(1)}, u32[]{:S(2)}, u32[]{:S(2)}) %collective-permute-start) | collective-permute-done | bytes 524320 | tf_op jit(solution)/shard_map/while/body/eval_jaxpr/ppermute | solution.py:19
  522.8 1.9 collective-permute-start
  524.7 27.1 %collective-permute-done = bf16[64,4096]{1,0:T(8,128)(2,1)S(1)} collective-permute-done((bf16[64,4096]{1,0:T(8,128)(2,1)S(1)}, bf16[64,4096]{1,0:T(8,128)(2,1)S(1)}, u32[]{:S(2)}, u32[]{:S(2)}) %collective-permute-start) | collective-permute-done | bytes 524320 | tf_op jit(solution)/shard_map/while/body/eval_jaxpr/ppermute | solution.py:19
  554.3 24.9 %collective-permute-done = bf16[64,4096]{1,0:T(8,128)(2,1)S(1)} collective-permute-done((bf16[64,4096]{1,0:T(8,128)(2,1)S(1)}, bf16[64,4096]{1,0:T(8,128)(2,1)S(1)}, u32[]{:S(2)}, u32[]{:S(2)}) %collective-permute-start) | collective-permute-done | bytes 524320 | tf_op jit(solution)/shard_map/while/body/eval_jaxpr/ppermute | solution.py:19
  581.6 24.8 %collective-permute-done = bf16[64,4096]{1,0:T(8,128)(2,1)S(1)} collective-permute-done((bf16[64,4096]{1,0:T(8,128)(2,1)S(1)}, bf16[64,4096]{1,0:T(8,128)(2,1)S(1)}, u32[]{:S(2)}, u32[]{:S(2)}) %collective-permute-start) | collective-permute-done | bytes 524320 | tf_op jit(solution)/shard_map/while/body/eval_jaxpr/ppermute | solution.py:19
  608.9 24.9 %collective-permute-done = bf16[64,4096]{1,0:T(8,128)(2,1)S(1)} collective-permute-done((bf16[64,4096]{1,0:T(8,128)(2,1)S(1)}, bf16[64,4096]{1,0:T(8,128)(2,1)S(1)}, u32[]{:S(2)}, u32[]{:S(2)}) %collective-permute-start) | collective-permute-done | bytes 524320 | tf_op jit(solution)/shard_map/while/body/eval_jaxpr/ppermute | solution.py:19
  636.1 24.8 %collective-permute-done = bf16[64,4096]{1,0:T(8,128)(2,1)S(1)} collective-permute-done((bf16[64,4096]{1,0:T(8,128)(2,1)S(1)}, bf16[64,4096]{1,0:T(8,128)(2,1)S(1)}, u32[]{:S(2)}, u32[]{:S(2)}) %collective-permute-start) | collective-permute-done | bytes 524320 | tf_op jit(solution)/shard_map/while/body/eval_jaxpr/ppermute | solution.py:19
  663.4 24.9 %collective-permute-done = bf16[64,4096]{1,0:T(8,128)(2,1)S(1)} collective-permute-done((bf16[64,4096]{1,0:T(8,128)(2,1)S(1)}, bf16[64,4096]{1,0:T(8,128)(2,1)S(1)}, u32[]{:S(2)}, u32[]{:S(2)}) %collective-permute-start) | collective-permute-done | bytes 524320 | tf_op jit(solution)/shard_map/while/body/eval_jaxpr/ppermute | solution.py:19
  690.7 24.8 %collective-permute-done = bf16[64,4096]{1,0:T(8,128)(2,1)S(1)} collective-permute-done((bf16[64,4096]{1,0:T(8,128)(2,1)S(1)}, bf16[64,4096]{1,0:T(8,128)(2,1)S(1)}, u32[]{:S(2)}, u32[]{:S(2)}) %collective-permute-start) | collective-permute-done | bytes 524320 | tf_op jit(solution)/shard_map/while/body/eval_jaxpr/ppermute | solution.py:19
  716.0 1.9 collective-permute-start
  718.0 24.9 %collective-permute-done = bf16[64,4096]{1,0:T(8,128)(2,1)S(1)} collective-permute-done((bf16[64,4096]{1,0:T(8,128)(2,1)S(1)}, bf16[64,4096]{1,0:T(8,128)(2,1)S(1)}, u32[]{:S(2)}, u32[]{:S(2)}) %collective-permute-start) | collective-permute-done | bytes 524320 | tf_op jit(solution)/shard_map/while/body/eval_jaxpr/ppermute | solution.py:19
  743.3 1.9 collective-permute-start
  745.2 24.8 %collective-permute-done = bf16[64,4096]{1,0:T(8,128)(2,1)S(1)} collective-permute-done((bf16[64,4096]{1,0:T(8,128)(2,1)S(1)}, bf16[64,4096]{1,0:T(8,128)(2,1)S(1)}, u32[]{:S(2)}, u32[]{:S(2)}) %collective-permute-start) | collective-permute-done | bytes 524320 | tf_op jit(solution)/shard_map/while/body/eval_jaxpr/ppermute | solution.py:19
  772.5 24.9 %collective-permute-done = bf16[64,4096]{1,0:T(8,128)(2,1)S(1)} collective-permute-done((bf16[64,4096]{1,0:T(8,128)(2,1)S(1)}, bf16[64,4096]{1,0:T(8,128)(2,1)S(1)}, u32[]{:S(2)}, u32[]{:S(2)}) %collective-permute-start) | collective-permute-done | bytes 524320 | tf_op jit(solution)/shard_map/while/body/eval_jaxpr/ppermute | solution.py:19
  797.8 1.9 collective-permute-start
  799.8 24.8 %collective-permute-done = bf16[64,4096]{1,0:T(8,128)(2,1)S(1)} collective-permute-done((bf16[64,4096]{1,0:T(8,128)(2,1)S(1)}, bf16[64,4096]{1,0:T(8,128)(2,1)S(1)}, u32[]{:S(2)}, u32[]{:S(2)}) %collective-permute-start) | collective-permute-done | bytes 524320 | tf_op jit(solution)/shard_map/while/body/eval_jaxpr/ppermute | solution.py:19
  825.1 1.9 collective-permute-start
  827.1 24.9 %collective-permute-done = bf16[64,4096]{1,0:T(8,128)(2,1)S(1)} collective-permute-done((bf16[64,4096]{1,0:T(8,128)(2,1)S(1)}, bf16[64,4096]{1,0:T(8,128)(2,1)S(1)}, u32[]{:S(2)}, u32[]{:S(2)}) %collective-permute-start) | collective-permute-done | bytes 524320 | tf_op jit(solution)/shard_map/while/body/eval_jaxpr/ppermute | solution.py:19
  (93 shorter events, 31.2 us)
Async XLA Ops:
  7.2 129.6 %copy-start = (bf16[512,64]{0,1:T(8,128)(2,1)S(1)}, bf16[512,64]{0,1:T(8,128)(2,1)}, u32[]{:S(2)}) copy-start(bf16[512,64]{0,1:T(8,128)(2,1)} %param.16) | copy-start | bytes 196612
  7.2 122.1 %copy-start.2 = (bf16[128,4096]{1,0:T(8,128)(2,1)S(1)}, bf16[128,4096]{1,0:T(8,128)(2,1)}, u32[]{:S(2)}) copy-start(bf16[128,4096]{1,0:T(8,128)(2,1)} %param.17) | copy-start | bytes 3145732
  7.2 173.6 %all-gather.6.cloned.1.call-start = ((), (), s32[]{:S(2)}) async-start(), calls=%async_computation.1 | async-start | bytes 1081344 | tf_op jit(solution)/shard_map/all_gather | solution.py:117
  7.9 122.7 %copy-start.3 = (bf16[128,4096]{1,0:T(8,128)(2,1)S(1)}, bf16[128,4096]{1,0:T(8,128)(2,1)}, u32[]{:S(2)}) copy-start(bf16[128,4096]{1,0:T(8,128)(2,1)} %param.19) | copy-start | bytes 3145732
  7.9 421.9 %all-gather.4.cloned.1.call-start = ((), (), s32[]{:S(2)}) async-start(), calls=%async_computation | async-start | bytes 8650752 | tf_op jit(solution)/shard_map/all_gather | solution.py:112
  130.6 1.5 copy-start.4
  134.3 2.6 copy-start.1
  434.5 2.5 copy-start.5
  434.5 2.9 copy-start.7
  438.7 28.5 %collective-permute-start = (bf16[64,4096]{1,0:T(8,128)(2,1)S(1)}, bf16[64,4096]{1,0:T(8,128)(2,1)S(1)}, u32[]{:S(2)}, u32[]{:S(2)}) collective-permute-start(bf16[64,4096]{1,0:T(8,128)(2,1)S(1)} %get-tuple-element.203), channel_id=1, source_target_pairs={{480,0},{0,32},{32,64},{64,96},{96,128},{128,160},{160,192},{192,2... | collective-permute-start | bytes 1572872 | tf_op jit(solution)/shard_map/while/body/eval_jaxpr/ppermute | solution.py:19
  467.7 22.8 %collective-permute-start = (bf16[64,4096]{1,0:T(8,128)(2,1)S(1)}, bf16[64,4096]{1,0:T(8,128)(2,1)S(1)}, u32[]{:S(2)}, u32[]{:S(2)}) collective-permute-start(bf16[64,4096]{1,0:T(8,128)(2,1)S(1)} %get-tuple-element.203), channel_id=1, source_target_pairs={{480,0},{0,32},{32,64},{64,96},{96,128},{128,160},{160,192},{192,2... | collective-permute-start | bytes 1572872 | tf_op jit(solution)/shard_map/while/body/eval_jaxpr/ppermute | solution.py:19
  491.1 31.3 %collective-permute-start = (bf16[64,4096]{1,0:T(8,128)(2,1)S(1)}, bf16[64,4096]{1,0:T(8,128)(2,1)S(1)}, u32[]{:S(2)}, u32[]{:S(2)}) collective-permute-start(bf16[64,4096]{1,0:T(8,128)(2,1)S(1)} %get-tuple-element.203), channel_id=1, source_target_pairs={{480,0},{0,32},{32,64},{64,96},{96,128},{128,160},{160,192},{192,2... | collective-permute-start | bytes 1572872 | tf_op jit(solution)/shard_map/while/body/eval_jaxpr/ppermute | solution.py:19
  522.8 29.0 %collective-permute-start = (bf16[64,4096]{1,0:T(8,128)(2,1)S(1)}, bf16[64,4096]{1,0:T(8,128)(2,1)S(1)}, u32[]{:S(2)}, u32[]{:S(2)}) collective-permute-start(bf16[64,4096]{1,0:T(8,128)(2,1)S(1)} %get-tuple-element.203), channel_id=1, source_target_pairs={{480,0},{0,32},{32,64},{64,96},{96,128},{128,160},{160,192},{192,2... | collective-permute-start | bytes 1572872 | tf_op jit(solution)/shard_map/while/body/eval_jaxpr/ppermute | solution.py:19
  552.3 26.9 %collective-permute-start = (bf16[64,4096]{1,0:T(8,128)(2,1)S(1)}, bf16[64,4096]{1,0:T(8,128)(2,1)S(1)}, u32[]{:S(2)}, u32[]{:S(2)}) collective-permute-start(bf16[64,4096]{1,0:T(8,128)(2,1)S(1)} %get-tuple-element.203), channel_id=1, source_target_pairs={{480,0},{0,32},{32,64},{64,96},{96,128},{128,160},{160,192},{192,2... | collective-permute-start | bytes 1572872 | tf_op jit(solution)/shard_map/while/body/eval_jaxpr/ppermute | solution.py:19
  579.6 26.8 %collective-permute-start = (bf16[64,4096]{1,0:T(8,128)(2,1)S(1)}, bf16[64,4096]{1,0:T(8,128)(2,1)S(1)}, u32[]{:S(2)}, u32[]{:S(2)}) collective-permute-start(bf16[64,4096]{1,0:T(8,128)(2,1)S(1)} %get-tuple-element.203), channel_id=1, source_target_pairs={{480,0},{0,32},{32,64},{64,96},{96,128},{128,160},{160,192},{192,2... | collective-permute-start | bytes 1572872 | tf_op jit(solution)/shard_map/while/body/eval_jaxpr/ppermute | solution.py:19
  606.9 26.8 %collective-permute-start = (bf16[64,4096]{1,0:T(8,128)(2,1)S(1)}, bf16[64,4096]{1,0:T(8,128)(2,1)S(1)}, u32[]{:S(2)}, u32[]{:S(2)}) collective-permute-start(bf16[64,4096]{1,0:T(8,128)(2,1)S(1)} %get-tuple-element.203), channel_id=1, source_target_pairs={{480,0},{0,32},{32,64},{64,96},{96,128},{128,160},{160,192},{192,2... | collective-permute-start | bytes 1572872 | tf_op jit(solution)/shard_map/while/body/eval_jaxpr/ppermute | solution.py:19
  634.2 26.8 %collective-permute-start = (bf16[64,4096]{1,0:T(8,128)(2,1)S(1)}, bf16[64,4096]{1,0:T(8,128)(2,1)S(1)}, u32[]{:S(2)}, u32[]{:S(2)}) collective-permute-start(bf16[64,4096]{1,0:T(8,128)(2,1)S(1)} %get-tuple-element.203), channel_id=1, source_target_pairs={{480,0},{0,32},{32,64},{64,96},{96,128},{128,160},{160,192},{192,2... | collective-permute-start | bytes 1572872 | tf_op jit(solution)/shard_map/while/body/eval_jaxpr/ppermute | solution.py:19
  661.5 26.8 %collective-permute-start = (bf16[64,4096]{1,0:T(8,128)(2,1)S(1)}, bf16[64,4096]{1,0:T(8,128)(2,1)S(1)}, u32[]{:S(2)}, u32[]{:S(2)}) collective-permute-start(bf16[64,4096]{1,0:T(8,128)(2,1)S(1)} %get-tuple-element.203), channel_id=1, source_target_pairs={{480,0},{0,32},{32,64},{64,96},{96,128},{128,160},{160,192},{192,2... | collective-permute-start | bytes 1572872 | tf_op jit(solution)/shard_map/while/body/eval_jaxpr/ppermute | solution.py:19
  688.7 26.8 %collective-permute-start = (bf16[64,4096]{1,0:T(8,128)(2,1)S(1)}, bf16[64,4096]{1,0:T(8,128)(2,1)S(1)}, u32[]{:S(2)}, u32[]{:S(2)}) collective-permute-start(bf16[64,4096]{1,0:T(8,128)(2,1)S(1)} %get-tuple-element.203), channel_id=1, source_target_pairs={{480,0},{0,32},{32,64},{64,96},{96,128},{128,160},{160,192},{192,2... | collective-permute-start | bytes 1572872 | tf_op jit(solution)/shard_map/while/body/eval_jaxpr/ppermute | solution.py:19
  716.0 26.8 %collective-permute-start = (bf16[64,4096]{1,0:T(8,128)(2,1)S(1)}, bf16[64,4096]{1,0:T(8,128)(2,1)S(1)}, u32[]{:S(2)}, u32[]{:S(2)}) collective-permute-start(bf16[64,4096]{1,0:T(8,128)(2,1)S(1)} %get-tuple-element.203), channel_id=1, source_target_pairs={{480,0},{0,32},{32,64},{64,96},{96,128},{128,160},{160,192},{192,2... | collective-permute-start | bytes 1572872 | tf_op jit(solution)/shard_map/while/body/eval_jaxpr/ppermute | solution.py:19
  743.3 26.8 %collective-permute-start = (bf16[64,4096]{1,0:T(8,128)(2,1)S(1)}, bf16[64,4096]{1,0:T(8,128)(2,1)S(1)}, u32[]{:S(2)}, u32[]{:S(2)}) collective-permute-start(bf16[64,4096]{1,0:T(8,128)(2,1)S(1)} %get-tuple-element.203), channel_id=1, source_target_pairs={{480,0},{0,32},{32,64},{64,96},{96,128},{128,160},{160,192},{192,2... | collective-permute-start | bytes 1572872 | tf_op jit(solution)/shard_map/while/body/eval_jaxpr/ppermute | solution.py:19
  770.6 26.8 %collective-permute-start = (bf16[64,4096]{1,0:T(8,128)(2,1)S(1)}, bf16[64,4096]{1,0:T(8,128)(2,1)S(1)}, u32[]{:S(2)}, u32[]{:S(2)}) collective-permute-start(bf16[64,4096]{1,0:T(8,128)(2,1)S(1)} %get-tuple-element.203), channel_id=1, source_target_pairs={{480,0},{0,32},{32,64},{64,96},{96,128},{128,160},{160,192},{192,2... | collective-permute-start | bytes 1572872 | tf_op jit(solution)/shard_map/while/body/eval_jaxpr/ppermute | solution.py:19
  797.8 26.8 %collective-permute-start = (bf16[64,4096]{1,0:T(8,128)(2,1)S(1)}, bf16[64,4096]{1,0:T(8,128)(2,1)S(1)}, u32[]{:S(2)}, u32[]{:S(2)}) collective-permute-start(bf16[64,4096]{1,0:T(8,128)(2,1)S(1)} %get-tuple-element.203), channel_id=1, source_target_pairs={{480,0},{0,32},{32,64},{64,96},{96,128},{128,160},{160,192},{192,2... | collective-permute-start | bytes 1572872 | tf_op jit(solution)/shard_map/while/body/eval_jaxpr/ppermute | solution.py:19
  825.1 26.8 %collective-permute-start = (bf16[64,4096]{1,0:T(8,128)(2,1)S(1)}, bf16[64,4096]{1,0:T(8,128)(2,1)S(1)}, u32[]{:S(2)}, u32[]{:S(2)}) collective-permute-start(bf16[64,4096]{1,0:T(8,128)(2,1)S(1)} %get-tuple-element.203), channel_id=1, source_target_pairs={{480,0},{0,32},{32,64},{64,96},{96,128},{128,160},{160,192},{192,2... | collective-permute-start | bytes 1572872 | tf_op jit(solution)/shard_map/while/body/eval_jaxpr/ppermute | solution.py:19
  852.4 0.6 copy-start.6
Sparse Core Ops, SparseCore 0:
  10.0 170.7 all-gather.5
  182.9 246.8 all-gather.3
where the time goes:
time: 872 us; the launch traced here: 860 us
  waiting for transfers between devices  645 us (74%)
  blocking collectives  118 us (14%)
  starting transfers between devices  51.9 us (6%)
  matrix products  18.8 us (2%)
  between operations  14.2 us (2%)
  local copies, waits for them, and re-layouts  9.19 us (1%)
    ppermute x15, waiting for transfers between devices, shifted(): return lax.ppermute(block, axis, route)  354 us
    all_gather x1, waiting for transfers between devices, on_device(): lax.all_gather(value_weight, 'fsdp', axis=0, tiled=True)  246 us
    all_gather x1, blocking collectives, circulate_scores(): start_block = lax.all_gather(query_grads, 'fsdp', axis=0, tiled=True)  118 us
    ppermute x15, starting transfers between devices, shifted(): return lax.ppermute(block, axis, route)  51.8 us
    all_gather x1, waiting for transfers between devices, on_device(): lax.all_gather(input_basis, 'fsdp', axis=0, tiled=True)  43.4 us
  transfers between devices with their start and end apart: 17, of which 17 were waited for; matrix products, arithmetic and copies ran while one was open for 2% of the time, Pallas kernels for 0%

commit v1 on v0

v1 whole, which is shorter than its diff:
```python
import math

import jax
import jax.numpy as jnp
from jax import lax
from jax.sharding import Mesh
from jax.sharding import PartitionSpec as P

HD = 128
GROUP = 8
KVH = 4
RANK = 64
LANES = 128

epsilon = 1e-05

AXES = ("zh", "x", "c", "y", "zl")
SIZES = (2, 4, 2, 4, 8)


def width(axes):
    return math.prod(lax.axis_size(a) for a in axes)


def exchange(blocks, axes):
    return lax.all_to_all(blocks, axes, 0, 0, tiled=False)


def spread(block, axes):
    return exchange(jnp.broadcast_to(block[None], (width(axes),) + block.shape), axes)


def segments(lengths, count):
    bounds = jnp.cumsum(lengths)
    places = jnp.arange(count, dtype=jnp.int32)
    return jnp.sum((places[:, None] >= bounds[None, :]).astype(jnp.int32), axis=1)


def attend(queries, keys, values, upstream, segment):
    count = queries.shape[0]
    places = jnp.arange(count, dtype=jnp.int32)
    query_heads = queries.reshape(count, KVH, GROUP, HD)
    key_heads = keys.reshape(count, KVH, HD)
    value_heads = values.reshape(count, KVH, HD)
    grad_heads = upstream.reshape(count, KVH, GROUP, HD)
    allowed = (segment[:, None] == segment[None, :]) & (places[None, :] <= places[:, None])
    scale = 1.0 / math.sqrt(HD)
    logits = (
        jnp.einsum("tjgd,ujd->jgtu", query_heads, key_heads, preferred_element_type=jnp.float32)
        * scale
    )
    logits = jnp.where(allowed, logits, jnp.float32(-1e30))
    row_max = jnp.max(logits, axis=-1, keepdims=True)
    expo = jnp.exp(logits - row_max)
    probs = expo / jnp.sum(expo, axis=-1, keepdims=True)
    probs_low = probs.astype(jnp.bfloat16)
    value_grad = jnp.einsum(
        "jgtu,tjgd->ujd", probs_low, grad_heads, preferred_element_type=jnp.float32
    ).astype(jnp.bfloat16)
    prob_grad = jnp.einsum(
        "tjgd,ujd->jgtu", grad_heads, value_heads, preferred_element_type=jnp.float32
    )
    logit_grad = probs * (prob_grad - jnp.sum(probs * prob_grad, axis=-1, keepdims=True))
    logit_low = logit_grad.astype(jnp.bfloat16)
    key_grad = (
        jnp.einsum("jgtu,tjgd->ujd", logit_low, query_heads, preferred_element_type=jnp.float32)
        * scale
    ).astype(jnp.bfloat16)
    return key_grad.reshape(count, KVH * HD), value_grad.reshape(count, KVH * HD)


def gather_weights(norm_gain, value_weight, input_basis):
    rows = value_weight.shape[0]
    half = rows // lax.axis_size("c")
    piece = half // lax.axis_size("x")
    shard = lax.axis_index("y") * lax.axis_size("zl") + lax.axis_index("zl")
    gain = lax.dynamic_slice_in_dim(norm_gain, shard * rows, rows, 0).astype(jnp.float32)
    both = jnp.concatenate([value_weight, input_basis], axis=1).astype(jnp.float32)
    both = (both * gain[:, None]).astype(jnp.bfloat16)
    begin = lax.axis_index("c") * half + lax.axis_index("x") * piece
    mine = lax.dynamic_slice_in_dim(both, begin, piece, 0)
    along_z = spread(mine, ("zl",))
    along_x = spread(along_z, ("x",))
    return along_x.transpose(1, 0, 2, 3).reshape(-1, both.shape[1])


def project(tokens, weights):
    count, features = tokens.shape
    cs, ys, zs = lax.axis_size("c"), lax.axis_size("y"), lax.axis_size("zl")
    piece = features // (cs * ys * zs)
    blocks = tokens.reshape(count, ys, zs, cs, piece).transpose(3, 1, 0, 2, 4)
    blocks = exchange(blocks.reshape(cs * ys, count, zs * piece), ("c", "y"))
    part = jnp.einsum("smk,kn->smn", blocks, weights, preferred_element_type=jnp.float32)
    wide = KVH * HD
    value_part, left_part = part[..., :wide], part[..., wide:]
    left_high = lax.reduce_precision(left_part, 8, 7)
    sent = jnp.concatenate([value_part, left_high, left_part - left_high], axis=2)
    came = exchange(sent.astype(jnp.bfloat16), ("c", "y")).astype(jnp.float32)
    total = jnp.sum(came, axis=0)
    return total[:, :wide], total[:, wide : wide + RANK] + total[:, wide + RANK :]


def gather_queries(query_grads):
    rows, length = query_grads.shape
    along_z = spread(query_grads, ("zh", "zl"))
    along_y = spread(along_z, ("y",))
    by_axis = along_y.reshape(
        lax.axis_size("y"), lax.axis_size("zh"), lax.axis_size("zl"), rows, length
    )
    return by_axis.transpose(1, 0, 2, 3, 4).reshape(-1, length)


def score(train_grads, some_queries):
    count = train_grads.shape[0]
    xs, cs, zhs = lax.axis_size("x"), lax.axis_size("c"), lax.axis_size("zh")
    others = spread(train_grads, ("x", "c")).reshape(xs * cs * count, -1)
    block = lax.dot_general(
        others, some_queries, (((1,), (1,)), ((), ())), preferred_element_type=jnp.float32
    )
    came = exchange(block.reshape(xs * cs, count, -1), ("x", "c"))
    came = came.reshape(xs, cs, count, zhs, -1)
    return came.transpose(2, 3, 0, 1, 4).reshape(count, -1)


def on_device(
    tokens,
    norm_gain,
    value_weight,
    input_basis,
    output_basis,
    rotated_queries,
    rotated_keys,
    upstream_grad,
    example_lengths,
    query_grads,
):
    some_queries = gather_queries(query_grads)
    weights = gather_weights(norm_gain, value_weight, input_basis)
    value_sum, left_sum = project(tokens, weights)
    activ = tokens.astype(jnp.float32)
    row_scale = lax.rsqrt(jnp.mean(activ * activ, axis=1, keepdims=True) + epsilon)
    values = (value_sum * row_scale).astype(jnp.bfloat16)
    left = left_sum * row_scale
    segment = segments(example_lengths[0], tokens.shape[0])
    key_grad, value_grad = attend(rotated_queries, rotated_keys, values, upstream_grad, segment)
    right = jnp.dot(value_grad, output_basis, preferred_element_type=jnp.float32)
    examples = example_lengths.shape[1]
    onehot = (segment[:, None] == jnp.arange(examples, dtype=jnp.int32)[None, :]).astype(jnp.float32)
    per_example = jnp.einsum("te,ti,tj->eij", onehot, left, right, precision=lax.Precision.HIGHEST)
    train_grads = per_example.reshape(examples, -1).astype(jnp.bfloat16)
    return (key_grad, score(train_grads, some_queries))


def solution(mesh):
    fine = Mesh(mesh.devices.reshape(SIZES), AXES)
    rows = P(AXES, None)
    return jax.shard_map(
        on_device,
        mesh=fine,
        in_specs=(
            rows,
            P(),
            P(("y", "zl"), None),
            P(("y", "zl"), None),
            P(),
            rows,
            rows,
            rows,
            rows,
            rows,
        ),
        out_specs=(rows, rows),
        check_vma=False,
    )
```

time: 872 us -> 187 us (0.21); the launches traced: 860 us -> 186 us
  waiting for transfers between devices: 645 us -> 49.8 us
  blocking collectives: 118 us -> 35.1 us
  local copies, waits for them, and re-layouts: 9.19 us -> 32 us
  between operations: 14.2 us -> 0.85 us
    ppermute x15 -> x0, waiting for transfers between devices: 354 us -> none  [shifted(): return lax.ppermute(block, axis, route)]
    all_gather x2 -> x0, waiting for transfers between devices: 289 us -> none  [the longest x1 246 us: on_device(): lax.all_gather(value_weight, 'fsdp', axis=0, tiled=True)]
    all_gather x1 -> x0, blocking collectives: 118 us -> none  [circulate_scores(): start_block = lax.all_gather(query_grads, 'fsdp', axis=0, tiled=True)]
    ppermute x15 -> x0, starting transfers between devices: 51.8 us -> none  [shifted(): return lax.ppermute(block, axis, route)]
    all_to_all x0 -> x7, waiting for transfers between devices: none -> 49.8 us  [exchange(): return lax.all_to_all(blocks, axes, 0, 0, tiled=False)]
    all_to_all x0 -> x7, starting transfers between devices: none -> 48.8 us  [exchange(): return lax.all_to_all(blocks, axes, 0, 0, tiled=False)]
    all_to_all x0 -> x1, blocking collectives: none -> 35.1 us  [exchange(): return lax.all_to_all(blocks, axes, 0, 0, tiled=False)]
    reshape x1 -> x6, local copies, waits for them, and re-layouts: 0.04 us -> 11.3 us  [the longest x2 5.88 us: project(): blocks = tokens.reshape(count, ys, zs, cs, piece).transpose(3, 1, 0, 2, 4)]
  transfers between devices with their start and end apart: 17 -> 7, of which waited for: 17 -> 7; matrix products, arithmetic and copies ran while one was open for 2% -> 22% of each run, Pallas kernels for 0% -> 0%
where the time goes in v1:
time: 187 us; the launch traced here: 186 us
  waiting for transfers between devices  49.8 us (27%)
  starting transfers between devices  48.8 us (26%)
  blocking collectives  35.1 us (19%)
  local copies, waits for them, and re-layouts  32 us (17%)
  matrix products  15.6 us (8%)
  other arithmetic  3.85 us (2%)
    all_to_all x7, waiting for transfers between devices, exchange(): return lax.all_to_all(blocks, axes, 0, 0, tiled=False)  49.8 us
    all_to_all x7, starting transfers between devices, exchange(): return lax.all_to_all(blocks, axes, 0, 0, tiled=False)  48.8 us
    all_to_all x1, blocking collectives, exchange(): return lax.all_to_all(blocks, axes, 0, 0, tiled=False)  35.1 us
    broadcast_in_dim x5, local copies, waits for them, and re-layouts, spread(): jnp.broadcast_to(block[None], (width(axes),) + block.shape)  6.64 us
    reshape x2, local copies, waits for them, and re-layouts, project(): blocks = tokens.reshape(count, ys, zs, cs, piece).transpose(3, 1, 0, 2, 4)  5.88 us
    reshape x1, local copies, waits for them, and re-layouts, project(): blocks = exchange(blocks.reshape(cs * ys, count, zs * piece), ('c', 'y'))  4.16 us
    dot_general x1, matrix products, attend(): jnp.einsum('tjgd,ujd->jgtu', grad_heads, value_heads, preferred_element_t...  3.8 us
  transfers between devices with their start and end apart: 7, of which 7 were waited for; matrix products, arithmetic and copies ran while one was open for 22% of the time, Pallas kernels for 0%

profile of v1, /device:TPU:1, one launch (start us, length us, event | category | flops | bytes accessed | tf_op | source)
XLA Modules:
  0.0 185.9 jit_solution(12248150342865493058)
XLA Ops:
  0.7 1.8 broadcast_in_dim.21
  2.4 15.7 %all-to-all-start.5 = ((bf16[16,2,4096]{2,1,0:T(2,128)(2,1)}), bf16[16,2,4096]{2,1,0:T(2,128)(2,1)S(1)}, u32[]{:S(2)}, u32[]{:S(2)}) async-start(bf16[16,2,4096]{2,1,0:T(2,128)(2,1)} %broadcast_in_dim.21), calls=%async_computation.5 | async-start | bytes 524288 | tf_op jit(solution)/shard_map/all_to_all | solution.py:26
  20.7 10.6 %all-to-all-done.5 = bf16[16,2,4096]{2,1,0:T(2,128)(2,1)S(1)} async-done(((bf16[16,2,4096]{2,1,0:T(2,128)(2,1)}), bf16[16,2,4096]{2,1,0:T(2,128)(2,1)S(1)}, u32[]{:S(2)}, u32[]{:S(2)}) %all-to-all-start.5) | async-done | bytes 262176 | tf_op jit(solution)/shard_map/all_to_all | solution.py:26
  32.1 10.8 %all-to-all-start = ((bf16[8,32,576]{2,1,0:T(8,128)(2,1)}), bf16[8,32,576]{2,1,0:T(8,128)(2,1)S(1)}, u32[]{:S(2)}, u32[]{:S(2)}) async-start(bf16[8,32,576]{2,1,0:T(8,128)(2,1)} %broadcast_in_dim.18), calls=%async_computation | async-start | bytes 655360 | tf_op jit(solution)/shard_map/all_to_all | solution.py:26
  43.0 2.7 %reshape.101 = bf16[128,4,8,2,128]{4,3,2,1,0:T(2,128)(2,1)} reshape(bf16[128,8192]{1,0:T(8,128)(2,1)S(1)} %copy-done.1) | data formatting | bytes 4194304 | tf_op jit(solution)/shard_map/reshape | solution.py:91
  45.7 3.2 %copy.98 = bf16[128,4,8,2,128]{4,2,0,1,3:T(8,128)(2,1)} copy(bf16[128,4,8,2,128]{4,3,2,1,0:T(2,128)(2,1)} %reshape.101) | data formatting | bytes 4194304 | tf_op jit(solution)/shard_map/reshape | solution.py:91
  48.9 4.2 %reshape.102 = bf16[8,128,1024]{2,1,0:T(8,128)(2,1)} reshape(bf16[2,4,128,8,128]{4,3,2,1,0:T(8,128)(2,1)} %bitcast.76) | data formatting | bytes 4194304 | tf_op jit(solution)/shard_map/reshape | solution.py:92
  53.0 5.7 %all-to-all-done = bf16[8,32,576]{2,1,0:T(8,128)(2,1)S(1)} async-done(((bf16[8,32,576]{2,1,0:T(8,128)(2,1)}), bf16[8,32,576]{2,1,0:T(8,128)(2,1)S(1)}, u32[]{:S(2)}, u32[]{:S(2)}) %all-to-all-start) | async-done | bytes 294944 | tf_op jit(solution)/shard_map/all_to_all | solution.py:26
  58.7 35.1 %all_to_all.40 = bf16[8,128,1024]{2,1,0:T(8,128)(2,1)} all-to-all(bf16[8,128,1024]{2,1,0:T(8,128)(2,1)} %reshape.102), channel_id=1, replica_groups=mesh['zh'=2,'x'=4,'c'=2,'y'=4,'zl'=8] {'c','y'}, dimensions={0} | all-to-all | bytes 4194304 | tf_op jit(solution)/shard_map/all_to_all | solution.py:26
  93.8 1.2 broadcast_in_dim.19
  95.0 4.1 %all-to-all-start.1 = ((bf16[4,8,32,576]{3,2,1,0:T(8,128)(2,1)}), bf16[4,8,32,576]{3,2,1,0:T(8,128)(2,1)S(1)}, u32[]{:S(2)}, u32[]{:S(2)}) async-start(bf16[4,8,32,576]{3,2,1,0:T(8,128)(2,1)} %broadcast_in_dim.19), calls=%async_computation.1 | async-start | bytes 2621440 | tf_op jit(solution)/shard_map/all_to_all | solution.py:26
  99.1 2.3 %copy.85 = bf16[128,4096]{0,1:T(8,128)(2,1)} copy(bf16[128,4096]{1,0:T(8,128)(2,1)} %param.15) | data formatting | bytes 2097152 | tf_op jit(solution)/shard_map/reshape | solution.py:42
  101.6 1.6 reshape.98
  103.4 1.8 copy.69
  105.2 11.3 %all-to-all-done.1 = bf16[4,8,32,576]{3,2,1,0:T(8,128)(2,1)S(1)} async-done(((bf16[4,8,32,576]{3,2,1,0:T(8,128)(2,1)}), bf16[4,8,32,576]{3,2,1,0:T(8,128)(2,1)S(1)}, u32[]{:S(2)}, u32[]{:S(2)}) %all-to-all-start.1) | async-done | bytes 1179680 | tf_op jit(solution)/shard_map/all_to_all | solution.py:26
  116.5 2.1 %broadcast_in_dim.22 = bf16[4,16,2,4096]{3,1,2,0:T(8,128)(2,1)} broadcast(bf16[16,2,4096]{2,0,1:T(8,128)(2,1)} %copy.69), dimensions={1,2,3} | broadcast | bytes 1310720 | tf_op jit(solution)/shard_map/broadcast_in_dim | solution.py:30
  118.5 4.2 %all-to-all-start.6 = ((bf16[4,16,2,4096]{3,1,2,0:T(8,128)(2,1)}), bf16[4,16,2,4096]{3,1,2,0:T(8,128)(2,1)}, u32[]{:S(2)}, u32[]{:S(2)}) async-start(bf16[4,16,2,4096]{3,1,2,0:T(8,128)(2,1)} %broadcast_in_dim.22), calls=%async_computation.6 | async-start | bytes 2097152 | tf_op jit(solution)/shard_map/all_to_all | solution.py:26
  122.8 3.4 %fusion.34 = (f32[4,8,128]{2,1,0:T(8,128)S(1)}, f32[4,8,128,128]{2,3,1,0:T(8,128)}) fusion(pred[128,128]{0,1:T(8,128)(4,1)S(1)} %fusion.26, bf16[128,4,8,128]{0,3,2,1:T(8,128)(2,1)} %bitcast.79, bf16[128,4,128,1]{2,1,0,3:T(4,128)(2,1)} %bitcast.85), kind=kOutput, calls=%fused_computation.55 | convolution fusion | flops 136315008 | bytes 3309568 | tf_op jit(solution)/shard_map/sub | solution.py:54
  126.2 2.3 %copy.86 = bf16[128,4096]{0,1:T(8,128)(2,1)} copy(bf16[128,4096]{1,0:T(8,128)(2,1)} %param.17) | data formatting | bytes 2097152 | tf_op jit(solution)/shard_map/reshape | solution.py:45
  128.6 1.4 copy-done.2
  130.1 1.7 convolution_bitcast_fusion
  133.2 3.3 %all-to-all-done.6 = bf16[4,16,2,4096]{3,1,2,0:T(8,128)(2,1)} async-done(((bf16[4,16,2,4096]{3,1,2,0:T(8,128)(2,1)}), bf16[4,16,2,4096]{3,1,2,0:T(8,128)(2,1)}, u32[]{:S(2)}, u32[]{:S(2)}) %all-to-all-start.6) | async-done | bytes 1048608 | tf_op jit(solution)/shard_map/all_to_all | solution.py:26
  136.5 5.9 %all-to-all-start.3 = ((bf16[8,128,640]{1,2,0:T(8,128)(2,1)}), bf16[8,128,640]{1,2,0:T(8,128)(2,1)S(1)}, u32[]{:S(2)}, u32[]{:S(2)}) async-start(bf16[8,128,640]{1,2,0:T(8,128)(2,1)} %pad_maximum_fusion), calls=%async_computation.3 | async-start | bytes 2621440 | tf_op jit(solution)/shard_map/all_to_all | solution.py:26
  142.4 2.3 %fusion.7 = bf16[4,128,128]{1,2,0:T(8,128)(2,1)S(1)} fusion(bf16[128,4,8,128]{0,3,2,1:T(8,128)(2,1)} %bitcast.81, f32[4,8,128,128]{2,3,1,0:T(8,128)} %get-tuple-element.13, f32[4,8,128]{2,1,0:T(8,128)S(1)} %get-tuple-element.12), kind=kOutput, calls=%fused_computation.20 | convolution fusion | flops 135331840 | bytes 3293184 | tf_op jit(solution)/shard_map/jgtu,tjgd->ujd/dot_general | solution.py:57
  145.4 2.3 %copy.70 = bf16[2,4,8,2,4096]{4,3,2,1,0:T(2,128)(2,1)S(1)} copy(bf16[2,4,8,2,4096]{4,2,0,3,1:T(8,128)(2,1)} %bitcast.23) | data formatting | bytes 2097152 | tf_op jit(solution)/shard_map/transpose | solution.py:110
  148.1 12.0 %all-to-all-done.3 = bf16[8,128,640]{1,2,0:T(8,128)(2,1)S(1)} async-done(((bf16[8,128,640]{1,2,0:T(8,128)(2,1)}), bf16[8,128,640]{1,2,0:T(8,128)(2,1)S(1)}, u32[]{:S(2)}, u32[]{:S(2)}) %all-to-all-start.3) | async-done | bytes 1310752 | tf_op jit(solution)/shard_map/all_to_all | solution.py:26
  161.8 3.8 %all-to-all-start.4 = ((bf16[8,8,4096]{2,1,0:T(8,128)(2,1)}), bf16[8,8,4096]{2,1,0:T(8,128)(2,1)S(1)}, u32[]{:S(2)}, u32[]{:S(2)}) async-start(bf16[8,8,4096]{2,1,0:T(8,128)(2,1)} %broadcast_in_dim.20), calls=%async_computation.4 | async-start | bytes 1048576 | tf_op jit(solution)/shard_map/all_to_all | solution.py:26
  165.6 3.8 %fusion.1 = (f32[4,8,128]{2,1,0:T(8,128)S(1)}, f32[4,128,128,8]{2,1,3,0:T(8,128)}) fusion(f32[4,8,128,128]{2,3,1,0:T(8,128)} %get-tuple-element.13, f32[4,8,128]{2,1,0:T(8,128)S(1)} %get-tuple-element.12, bf16[128,4,128,1]{0,2,3,1:T(8,128)(2,1)S(1)} %bitcast.86, bf16[128,4,8,128]{0,3,2,1:T(8,128)(2,1)} %bitcast.82), kind=kOutput, calls=%fused_computation.6 | convolution fusion | flops 135786496 | bytes 5406720 | tf_op jit(solution)/shard_map/tjgd,ujd->jgtu/dot_general | solution.py:60
  169.4 5.7 %all-to-all-done.4 = bf16[8,8,4096]{2,1,0:T(8,128)(2,1)S(1)} async-done(((bf16[8,8,4096]{2,1,0:T(8,128)(2,1)}), bf16[8,8,4096]{2,1,0:T(8,128)(2,1)S(1)}, u32[]{:S(2)}, u32[]{:S(2)}) %all-to-all-start.4) | async-done | bytes 524320 | tf_op jit(solution)/shard_map/all_to_all | solution.py:26
  176.2 4.1 %all-to-all-start.7 = ((f32[8,8,128]{2,1,0:T(8,128)}), f32[8,8,128]{2,1,0:T(8,128)S(1)}, u32[]{:S(2)}, u32[]{:S(2)}) async-start(f32[8,8,128]{2,1,0:T(8,128)} %fusion.37), calls=%async_computation.7 | async-start | bytes 65536 | tf_op jit(solution)/shard_map/all_to_all | solution.py:26
  180.3 2.7 %fusion.6 = bf16[4,128,128]{1,2,0:T(8,128)(2,1)S(1)} fusion(bf16[128,4,8,128]{0,3,2,1:T(8,128)(2,1)S(1)} %bitcast.80, f32[4,128,128,8]{2,1,3,0:T(8,128)} %get-tuple-element.15, f32[4,8,128]{2,1,0:T(8,128)S(1)} %get-tuple-element.14, f32[4,8,128,128]{2,3,1,0:T(8,128)} %get-tuple-element.13, f32[4,8,128]{2,1,0:T(8,128)S(1)} %get-tuple-element.12), kind=kOutput, calls=%fused_computation.18 | convolution fusion | flops 136445952 | bytes 5406720 | tf_op jit(solution)/shard_map/jgtu,tjgd->ujd/dot_general | solution.py:66
  183.8 1.2 all-to-all-done.7
  (40 shorter events, 10.7 us)
Async XLA Ops:
  0.6 144.1 %copy-start = (bf16[512,64]{0,1:T(8,128)(2,1)S(1)}, bf16[512,64]{0,1:T(8,128)(2,1)}, u32[]{:S(2)}) copy-start(bf16[512,64]{0,1:T(8,128)(2,1)} %param.14) | copy-start | bytes 196612
  0.6 42.3 %copy-start.1 = (bf16[128,8192]{1,0:T(8,128)(2,1)S(1)}, bf16[128,8192]{1,0:T(8,128)(2,1)}, u32[]{:S(2)}) copy-start(bf16[128,8192]{1,0:T(8,128)(2,1)} %param.10) | copy-start | bytes 6291460
  2.4 28.9 %all-to-all-start.5 = ((bf16[16,2,4096]{2,1,0:T(2,128)(2,1)}), bf16[16,2,4096]{2,1,0:T(2,128)(2,1)S(1)}, u32[]{:S(2)}, u32[]{:S(2)}) async-start(bf16[16,2,4096]{2,1,0:T(2,128)(2,1)} %broadcast_in_dim.21), calls=%async_computation.5 | async-start | bytes 524288 | tf_op jit(solution)/shard_map/all_to_all | solution.py:26
  31.3 0.8 copy-start.4
  32.1 26.6 %all-to-all-start = ((bf16[8,32,576]{2,1,0:T(8,128)(2,1)}), bf16[8,32,576]{2,1,0:T(8,128)(2,1)S(1)}, u32[]{:S(2)}, u32[]{:S(2)}) async-start(bf16[8,32,576]{2,1,0:T(8,128)(2,1)} %broadcast_in_dim.18), calls=%async_computation | async-start | bytes 655360 | tf_op jit(solution)/shard_map/all_to_all | solution.py:26
  95.0 6.4 %copy-start.5 = (s32[1,8]{1,0:T(1,128)S(1)}, s32[1,8]{1,0:T(1,128)}, u32[]{:S(2)}) copy-start(s32[1,8]{1,0:T(1,128)} %param.18) | copy-start | bytes 100
  95.0 21.5 %all-to-all-start.1 = ((bf16[4,8,32,576]{3,2,1,0:T(8,128)(2,1)}), bf16[4,8,32,576]{3,2,1,0:T(8,128)(2,1)S(1)}, u32[]{:S(2)}, u32[]{:S(2)}) async-start(bf16[4,8,32,576]{3,2,1,0:T(8,128)(2,1)} %broadcast_in_dim.19), calls=%async_computation.1 | async-start | bytes 2621440 | tf_op jit(solution)/shard_map/all_to_all | solution.py:26
  118.5 17.9 %all-to-all-start.6 = ((bf16[4,16,2,4096]{3,1,2,0:T(8,128)(2,1)}), bf16[4,16,2,4096]{3,1,2,0:T(8,128)(2,1)}, u32[]{:S(2)}, u32[]{:S(2)}) async-start(bf16[4,16,2,4096]{3,1,2,0:T(8,128)(2,1)} %broadcast_in_dim.22), calls=%async_computation.6 | async-start | bytes 2097152 | tf_op jit(solution)/shard_map/all_to_all | solution.py:26
  128.5 1.6 copy-start.2
  136.5 23.7 %all-to-all-start.3 = ((bf16[8,128,640]{1,2,0:T(8,128)(2,1)}), bf16[8,128,640]{1,2,0:T(8,128)(2,1)S(1)}, u32[]{:S(2)}, u32[]{:S(2)}) async-start(bf16[8,128,640]{1,2,0:T(8,128)(2,1)} %pad_maximum_fusion), calls=%async_computation.3 | async-start | bytes 2621440 | tf_op jit(solution)/shard_map/all_to_all | solution.py:26
  161.8 13.3 %all-to-all-start.4 = ((bf16[8,8,4096]{2,1,0:T(8,128)(2,1)}), bf16[8,8,4096]{2,1,0:T(8,128)(2,1)S(1)}, u32[]{:S(2)}, u32[]{:S(2)}) async-start(bf16[8,8,4096]{2,1,0:T(8,128)(2,1)} %broadcast_in_dim.20), calls=%async_computation.4 | async-start | bytes 1048576 | tf_op jit(solution)/shard_map/all_to_all | solution.py:26
  165.6 14.7 %copy-start.3 = (bf16[128,4096]{0,1:T(8,128)(2,1)S(1)}, bf16[128,4096]{0,1:T(8,128)(2,1)}, u32[]{:S(2)}) copy-start(bf16[128,4096]{0,1:T(8,128)(2,1)} %copy.85) | copy-start | bytes 3145732
  176.2 8.9 %all-to-all-start.7 = ((f32[8,8,128]{2,1,0:T(8,128)}), f32[8,8,128]{2,1,0:T(8,128)S(1)}, u32[]{:S(2)}, u32[]{:S(2)}) async-start(f32[8,8,128]{2,1,0:T(8,128)} %fusion.37), calls=%async_computation.7 | async-start | bytes 65536 | tf_op jit(solution)/shard_map/all_to_all | solution.py:26

commit v2 on v1

v2 whole, which is shorter than its diff:
```python
import math

import jax
import jax.numpy as jnp
from jax import lax
from jax.experimental import pallas as pl
from jax.experimental.pallas import tpu as pltpu
from jax.sharding import Mesh
from jax.sharding import PartitionSpec as P

HD = 128
GROUP = 8
KVH = 4
RANK = 64
LANES = 128
QUERY_ROWS = 16

epsilon = 1e-05

AXES = ("zh", "x", "c", "y", "zl")
SIZES = (2, 4, 2, 4, 8)


def width(axes):
    return math.prod(lax.axis_size(a) for a in axes)


def exchange(blocks, axes):
    return lax.all_to_all(blocks, axes, 0, 0, tiled=False)


def spread(block, axes):
    return exchange(jnp.broadcast_to(block[None], (width(axes),) + block.shape), axes)


def segments(lengths, count):
    bounds = jnp.cumsum(lengths)
    places = jnp.arange(count, dtype=jnp.int32)
    return jnp.sum((places[:, None] >= bounds[None, :]).astype(jnp.int32), axis=1)


def attend_probs(queries, keys, upstream, segment):
    count = queries.shape[0]
    places = jnp.arange(count, dtype=jnp.int32)
    query_heads = queries.reshape(count, KVH, GROUP, HD)
    key_heads = keys.reshape(count, KVH, HD)
    grad_heads = upstream.reshape(count, KVH, GROUP, HD)
    allowed = (segment[:, None] == segment[None, :]) & (places[None, :] <= places[:, None])
    scale = 1.0 / math.sqrt(HD)
    logits = (
        jnp.einsum("tjgd,ujd->jgtu", query_heads, key_heads, preferred_element_type=jnp.float32)
        * scale
    )
    logits = jnp.where(allowed, logits, jnp.float32(-1e30))
    row_max = jnp.max(logits, axis=-1, keepdims=True)
    expo = jnp.exp(logits - row_max)
    probs = expo / jnp.sum(expo, axis=-1, keepdims=True)
    value_grad = jnp.einsum(
        "jgtu,tjgd->ujd",
        probs.astype(jnp.bfloat16),
        grad_heads,
        preferred_element_type=jnp.float32,
    ).astype(jnp.bfloat16)
    return probs, value_grad.reshape(count, KVH * HD)


def attend_keys(queries, probs, values, upstream):
    count = queries.shape[0]
    query_heads = queries.reshape(count, KVH, GROUP, HD)
    value_heads = values.reshape(count, KVH, HD)
    grad_heads = upstream.reshape(count, KVH, GROUP, HD)
    prob_grad = jnp.einsum(
        "tjgd,ujd->jgtu", grad_heads, value_heads, preferred_element_type=jnp.float32
    )
    logit_grad = probs * (prob_grad - jnp.sum(probs * prob_grad, axis=-1, keepdims=True))
    logit_low = logit_grad.astype(jnp.bfloat16)
    key_grad = jnp.einsum("jgtu,tjgd->ujd", logit_low, query_heads, preferred_element_type=jnp.float32)
    return (key_grad * (1.0 / math.sqrt(HD))).astype(jnp.bfloat16).reshape(count, KVH * HD)


def spec(space):
    return pl.BlockSpec(memory_space=space)


def local_kernel(body, out_shape, scratch=(), flops=0, moved=0):
    def call(place, *arrays):
        return pl.pallas_call(
            body,
            out_shape=out_shape,
            in_specs=[spec(pltpu.SMEM)] + [spec(pltpu.VMEM)] * len(arrays),
            out_specs=jax.tree.map(lambda _: spec(pltpu.VMEM), out_shape),
            scratch_shapes=scratch,
            compiler_params=pltpu.CompilerParams(vmem_limit_bytes=40 * 1024 * 1024),
            cost_estimate=pl.CostEstimate(flops=flops, bytes_accessed=moved, transcendentals=0),
        )(place, *arrays)

    return call


def scaled_weights_kernel(place, gain, values, basis, out, turned):
    c, x, block = place[0], place[1], place[2]
    rows = pl.ds(pl.multiple_of(c * LANES, LANES), LANES)
    mine = lax.broadcasted_iota(jnp.int32, gain.shape, 0) == block
    factor = jnp.sum(jnp.where(mine, gain[...].astype(jnp.float32), 0.0), axis=0, keepdims=True)
    head = values[rows, pl.ds(pl.multiple_of(x * HD, HD), HD)].astype(jnp.float32)
    turned[...] = basis[rows, :].astype(jnp.float32).T
    share = out.shape[1] - HD
    some = turned[pl.ds(pl.multiple_of(x * share, share), share), :]
    piece = jnp.concatenate([head.T, some], axis=0) * factor
    out[...] = jnp.broadcast_to(piece.astype(out.dtype)[None], out.shape)


def gather_weights(norm_gain, value_weight, input_basis):
    c, x = lax.axis_index("c"), lax.axis_index("x")
    zs = lax.axis_size("zl")
    shard = lax.axis_index("y") * zs + lax.axis_index("zl")
    place = jnp.stack([c, x, shard * lax.axis_size("c") + c]).astype(jnp.int32)
    share = RANK // lax.axis_size("x")
    sent = local_kernel(
        scaled_weights_kernel,
        jax.ShapeDtypeStruct((zs, HD + share, LANES), jnp.bfloat16),
        (pltpu.VMEM((RANK, LANES), jnp.float32),),
        moved=1 << 20,
    )(place, norm_gain.reshape(-1, LANES), value_weight, input_basis)
    return exchange(sent, ("zl",))


def swapped(block):
    return lax.ppermute(block, "c", [(0, 1), (1, 0)])


def share_tokens(tokens):
    ys = lax.axis_size("y")
    features = tokens.shape[1] // ys
    blocks = []
    for s in range(ys):
        target = lax.rem(lax.axis_index("y") + s, ys)
        block = lax.dynamic_slice_in_dim(tokens, target * features, features, 1)
        if s:
            block = lax.ppermute(block, "y", [(i, (i + s) % ys) for i in range(ys)])
        blocks.append(block)
    return blocks


def lay_out(weights, whole):
    xs, zs, width_, depth = weights.shape
    share = width_ - HD
    for x in range(xs):
        for z in range(zs):
            features = slice(z * depth, (z + 1) * depth)
            whole[x * HD : (x + 1) * HD, features] = weights[x, z, :HD, :]
            begin = xs * HD + x * share
            whole[begin : begin + share, features] = weights[x, z, HD:, :]


def half_product(half, weights, blocks, rows, whole):
    lay_out(weights, whole)
    count, depth = blocks[0].shape[0], weights.shape[3]
    for distance, block in enumerate(blocks):
        for z in range(weights.shape[1]):
            begin = pl.multiple_of((2 * z + half) * depth, depth)
            rows[distance * count : (distance + 1) * count, z * depth : (z + 1) * depth] = block[
                :, pl.ds(begin, depth)
            ]
    return lax.dot_general(
        rows[...], whole[...], (((1,), (1,)), ((), ())), preferred_element_type=jnp.float32
    )


def own_half_kernel(place, weights, *refs):
    *blocks, out, rows, whole = refs
    out[...] = half_product(place[1], weights, blocks, rows, whole)


def partner_half_kernel(place, weights, begun, *refs):
    *blocks, out, rows, whole = refs
    count, wide, ys = blocks[0].shape[0], KVH * HD, len(blocks)
    total = begun[...] + half_product(1 - place[1], weights, blocks, rows, whole)
    left = total[:, wide:]
    high = left.astype(jnp.bfloat16)
    low = (left - high.astype(jnp.float32)).astype(jnp.bfloat16)
    sent = jnp.concatenate([total[:, :wide].astype(jnp.bfloat16), high, low], axis=1)
    for distance in range(ys):
        out[lax.rem(place[0] - distance + ys, ys)] = sent[distance * count : (distance + 1) * count]


def project(blocks, weights):
    ys, count = len(blocks), blocks[0].shape[0]
    xs, zs, width_, depth = weights.shape
    columns = xs * width_
    place = jnp.stack([lax.axis_index("y"), lax.axis_index("c")]).astype(jnp.int32)
    scratch = (
        pltpu.VMEM((ys * count, zs * depth), jnp.bfloat16),
        pltpu.VMEM((columns, zs * depth), jnp.bfloat16),
    )
    cost = dict(flops=2 * ys * count * columns * zs * depth, moved=4 << 20)
    part = jax.ShapeDtypeStruct((ys * count, columns), jnp.float32)
    begun = local_kernel(own_half_kernel, part, scratch, **cost)(place, weights, *blocks)
    sent = jax.ShapeDtypeStruct((ys, count, columns + RANK), jnp.bfloat16)
    other = swapped(weights)
    return local_kernel(partner_half_kernel, sent, scratch, **cost)(place, other, begun, *blocks)


def spread_along_z(query_grads):
    rows = query_grads.shape[0]
    sent = jnp.pad(query_grads, ((0, QUERY_ROWS - rows), (0, 0)))
    return lax.all_gather(sent, ("zh", "zl"), axis=0, tiled=False)[:, :rows]


def spread_along_y(some_queries):
    ys = lax.axis_size("y")
    return jnp.concatenate(
        [some_queries]
        + [lax.ppermute(some_queries, "y", [(i, (i + s) % ys) for i in range(ys)]) for s in range(1, ys)],
        axis=0,
    )


def query_order(rows):
    zhs, ys, zs = (lax.axis_size(a) for a in ("zh", "y", "zl"))
    n = jnp.arange(zhs * ys * zs * rows, dtype=jnp.int32)
    row, zl, y, zh = n % rows, n // rows % zs, n // (rows * zs) % ys, n // (rows * zs * ys)
    distance = (lax.axis_index("y").astype(jnp.int32) - y) % ys
    k = ((distance * zhs + zh) * zs + zl) * rows + row
    return (n[:, None] == k[None, :]).astype(jnp.float32)


def score(others, some_queries, pick):
    xs, cs, zhs = lax.axis_size("x"), lax.axis_size("c"), lax.axis_size("zh")
    count = others.shape[1]
    block = lax.dot_general(
        others.reshape(xs * cs * count, -1),
        some_queries,
        (((1,), (1,)), ((), ())),
        preferred_element_type=jnp.float32,
    )
    block = jnp.dot(block, pick, precision=lax.Precision.HIGHEST)
    came = exchange(block.reshape(xs * cs, count, -1), ("x", "c"))
    came = came.reshape(xs, cs, count, zhs, -1)
    return came.transpose(2, 3, 0, 1, 4).reshape(count, -1)


def on_device(
    tokens,
    norm_gain,
    value_weight,
    input_basis,
    output_basis,
    rotated_queries,
    rotated_keys,
    upstream_grad,
    example_lengths,
    query_grads,
):
    some_queries = spread_along_z(query_grads)
    along_z = gather_weights(norm_gain, value_weight, input_basis)
    token_blocks = share_tokens(tokens)
    segment = segments(example_lengths[0], tokens.shape[0])
    probs, value_grad = attend_probs(rotated_queries, rotated_keys, upstream_grad, segment)
    right = jnp.dot(value_grad, output_basis, preferred_element_type=jnp.float32)
    along_z, right, token_blocks[1], token_blocks[-1] = lax.optimization_barrier(
        (along_z, right, token_blocks[1], token_blocks[-1])
    )

    weights = spread(along_z, ("x",))
    activ = tokens.astype(jnp.float32)
    row_scale = lax.rsqrt(jnp.mean(activ * activ, axis=1, keepdims=True) + epsilon)
    weights, row_scale, *token_blocks = lax.optimization_barrier((weights, row_scale, *token_blocks))

    came = exchange(project(token_blocks, weights), ("y",))
    pick = query_order(query_grads.shape[0])
    came, pick = lax.optimization_barrier((came, pick))
    total = jnp.sum(came.astype(jnp.float32), axis=0)
    wide = KVH * HD
    values = (total[:, :wide] * row_scale).astype(jnp.bfloat16)
    left = (total[:, wide : wide + RANK] + total[:, wide + RANK :]) * row_scale

    examples = example_lengths.shape[1]
    onehot = (segment[:, None] == jnp.arange(examples, dtype=jnp.int32)[None, :]).astype(jnp.float32)
    per_example = jnp.einsum("te,ti,tj->eij", onehot, left, right, precision=lax.Precision.HIGHEST)
    train_grads = per_example.reshape(examples, -1).astype(jnp.bfloat16)
    others = spread(train_grads, ("x", "c"))
    gathered = spread_along_y(some_queries.reshape(-1, some_queries.shape[-1]))
    key_grad = attend_keys(rotated_queries, probs, values, upstream_grad)
    others, gathered = lax.optimization_barrier((others, gathered))
    return (key_grad, score(others, gathered, pick))


def solution(mesh):
    fine = Mesh(mesh.devices.reshape(SIZES), AXES)
    rows = P(AXES, None)
    return jax.shard_map(
        on_device,
        mesh=fine,
        in_specs=(
            rows,
            P(),
            P(("y", "zl"), None),
            P(("y", "zl"), None),
            P(),
            rows,
            rows,
            rows,
            rows,
            rows,
        ),
        out_specs=(rows, rows),
        check_vma=False,
    )
```

time: 187 us -> 145 us (0.78)
  blocking collectives: 35.1 us -> 0 us
  waiting for transfers between devices: 49.8 us -> 25.5 us
  starting transfers between devices: 48.8 us -> 65.1 us
  local copies, waits for them, and re-layouts: 32 us -> 17.1 us
  between operations: 0.85 us -> 14.4 us
  Pallas kernels: 0 us -> 5.72 us
  matrix products: 15.6 us -> 13.6 us
    all_to_all x7 -> x5, waiting for transfers between devices: 49.8 us -> 11.8 us  [exchange(): return lax.all_to_all(blocks, axes, 0, 0, tiled=False)]
    all_to_all x1 -> x0, blocking collectives: 35.1 us -> none  [exchange(): return lax.all_to_all(blocks, axes, 0, 0, tiled=False)]
    ppermute x0 -> x7, starting transfers between devices: none -> 23.8 us  [the longest x3 10.1 us: share_tokens(): block = lax.ppermute(block, 'y', [(i, (i + s) % ys) for i in range(ys)])]
    reshape x7 -> x3, local copies, waits for them, and re-layouts: 16.6 us -> 3.11 us  [the longest x1 1.68 us: attend_probs(): key_heads = keys.reshape(count, KVH, HD)]
    ppermute x0 -> x7, waiting for transfers between devices: none -> 13.5 us  [the longest x3 9.65 us: share_tokens(): block = lax.ppermute(block, 'y', [(i, (i + s) % ys) for i in range(ys)])]
    all_to_all x7 -> x5, starting transfers between devices: 48.8 us -> 41.3 us  [exchange(): return lax.all_to_all(blocks, axes, 0, 0, tiled=False)]
    pallas_call x0 -> x3, Pallas kernels: none -> 5.72 us  [call(): pl.pallas_call(body, out_shape=out_shape, in_specs=[spec(pltpu.SMEM)] + [...]
    broadcast_in_dim x5 -> x2, local copies, waits for them, and re-layouts: 6.64 us -> 1.99 us  [spread(): jnp.broadcast_to(block[None], (width(axes),) + block.shape)]
  transfers between devices with their start and end apart: 7 -> 13, of which waited for: 7 -> 7; matrix products, arithmetic and copies ran while one was open for 22% -> 20% of each run, Pallas kernels for 0% -> 3%
where the time goes in v2:
time: 145 us; the launch traced here: 144 us
  starting transfers between devices  65.1 us (45%)
  waiting for transfers between devices  25.5 us (18%)
  local copies, waits for them, and re-layouts  17.1 us (12%)
  between operations  14.4 us (10%)
  matrix products  13.6 us (9%)
  Pallas kernels  5.72 us (4%)
  other arithmetic  3 us (2%)
    all_to_all x5, starting transfers between devices, exchange(): return lax.all_to_all(blocks, axes, 0, 0, tiled=False)  41.3 us
    all_to_all x5, waiting for transfers between devices, exchange(): return lax.all_to_all(blocks, axes, 0, 0, tiled=False)  11.8 us
    ppermute x3, starting transfers between devices, share_tokens(): block = lax.ppermute(block, 'y', [(i, (i + s) % ys) for i in range(ys)])  10.1 us
    ppermute x3, waiting for transfers between devices, share_tokens(): block = lax.ppermute(block, 'y', [(i, (i + s) % ys) for i in range(ys)])  9.65 us
    ppermute x3, starting transfers between devices, spread_along_y(): lax.ppermute(some_queries, 'y', [(i, (i + s) % ys) for i in range(ys)])  9.14 us
    unnamed x25, local copies, waits for them, and re-layouts  5.83 us
    pallas_call x3, Pallas kernels, call(): pl.pallas_call(body, out_shape=out_shape, in_specs=[spec(pltpu.SMEM)] + [...  5.72 us
    ppermute x1, starting transfers between devices, swapped(): return lax.ppermute(block, 'c', [(0, 1), (1, 0)])  4.55 us
  transfers between devices with their start and end apart: 13, of which 7 were waited for; matrix products, arithmetic and copies ran while one was open for 20% of the time, Pallas kernels for 3%

profile of v2, /device:TPU:1, one launch (start us, length us, event | category | flops | bytes accessed | tf_op | source)
XLA Modules:
  0.0 144.4 jit_solution(11722131558034022184)
XLA Ops:
  7.2 0.9 copy.50.basis
  8.2 0.9 copy-done.1
  9.9 1.4 shard_map.113
  11.2 13.1 %all-to-all-start = ((bf16[8,144,128]{2,1,0:T(8,128)(2,1)}), bf16[8,144,128]{2,1,0:T(8,128)(2,1)S(1)}, u32[]{:S(2)}, u32[]{:S(2)}) async-start(bf16[8,144,128]{2,1,0:T(8,128)(2,1)} %shard_map.113), calls=%async_computation | async-start | bytes 589824 | tf_op jit(solution)/shard_map/all_to_all | solution.py:29
  24.4 2.8 %constant_dynamic-slice_fusion = (bf16[128,2048]{1,0:T(8,128)(2,1)}, bf16[128,2048]{1,0:T(8,128)(2,1)S(1)}, bf16[128,2048]{1,0:T(8,128)(2,1)}, bf16[128,2048]{1,0:T(8,128)(2,1)S(1)}) fusion(bf16[128,8192]{1,0:T(8,128)(2,1)} %param.10, s32[]{:T(128)S(6)} %select_n.78, s32[]{:T(128)S(6)} %select_n.76, s32[]{:T(128)S(6)} %select_n.75, s32[]{:T(128)S(6)} %select_n.77), kind=kLoop, calls=%fused_computation.66 | loop fusion | bytes 4194320 | tf_op jit(solution)/shard_map/dynamic_slice | solution.py:138
  27.2 3.2 %collective-permute-start = (bf16[128,2048]{1,0:T(8,128)(2,1)}, bf16[128,2048]{1,0:T(8,128)(2,1)S(1)}, u32[]{:S(2)}, u32[]{:S(2)}) collective-permute-start(bf16[128,2048]{1,0:T(8,128)(2,1)} %get-tuple-element.40), channel_id=1, source_target_pairs={{0,8},{8,16},{16,24},{24,0},{1,9},{9,17},{17,25},{25,1},{2,10},{10... | collective-permute-start | bytes 1572872 | tf_op jit(solution)/shard_map/ppermute | solution.py:140
  30.4 3.4 %collective-permute-start.1 = (bf16[128,2048]{1,0:T(8,128)(2,1)S(1)}, bf16[128,2048]{1,0:T(8,128)(2,1)S(1)}, u32[]{:S(2)}, u32[]{:S(2)}) collective-permute-start(bf16[128,2048]{1,0:T(8,128)(2,1)S(1)} %get-tuple-element.39), channel_id=1, source_target_pairs={{0,24},{8,0},{16,8},{24,16},{1,25},{9,1},{17,9},{25,17},{2,26},{10... | collective-permute-start | bytes 1572872 | tf_op jit(solution)/shard_map/ppermute | solution.py:140
  34.9 1.3 copy.72
  36.2 1.7 %reshape.178 = bf16[128,4,128]{2,1,0:T(4,128)(2,1)} reshape(bf16[128,512]{1,0:T(8,128)(2,1)} %param.16) | data formatting | bytes 262144 | tf_op jit(solution)/shard_map/reshape | solution.py:46
  37.9 2.4 %copy.73 = bf16[16,8,32,128]{3,2,1,0:T(8,128)(2,1)} copy(bf16[16,8,32,128]{3,1,2,0:T(8,128)(2,1)} %bitcast.78) | data formatting | bytes 2097152
  40.4 3.0 %fusion.50 = (f32[4,8,128]{2,1,0:T(8,128)S(1)}, f32[4,8,128,128]{2,3,1,0:T(8,128)}) fusion(pred[128,128]{0,1:T(8,128)(4,1)S(1)} %fusion.31, bf16[128,4,8,128]{0,3,2,1:T(8,128)(2,1)S(1)} %bitcast.79, bf16[128,4,128,1]{2,1,0,3:T(4,128)(2,1)} %bitcast.87), kind=kOutput, calls=%fused_computation.90 | convolution fusion | flops 136315008 | bytes 3309568 | tf_op jit(solution)/shard_map/sub | solution.py:56
  43.4 2.5 %fusion.7 = bf16[4,128,128]{1,2,0:T(8,128)(2,1)S(1)} fusion(bf16[128,4,8,128]{3,2,1,0:T(8,128)(2,1)} %bitcast.81, f32[4,8,128,128]{2,3,1,0:T(8,128)} %get-tuple-element.43, f32[4,8,128]{2,1,0:T(8,128)S(1)} %get-tuple-element.42), kind=kOutput, calls=%fused_computation.16 | convolution fusion | flops 135331840 | bytes 3293184 | tf_op jit(solution)/shard_map/jgtu,tjgd->ujd/dot_general | solution.py:58
  46.1 1.2 broadcast_in_dim.14
  47.3 4.0 %all-to-all-start.1 = ((bf16[4,8,144,128]{3,2,1,0:T(8,128)(2,1)}), bf16[4,8,144,128]{3,2,1,0:T(8,128)(2,1)S(1)}, u32[]{:S(2)}, u32[]{:S(2)}) async-start(bf16[4,8,144,128]{3,2,1,0:T(8,128)(2,1)} %broadcast_in_dim.14), calls=%async_computation.1 | async-start | bytes 2359296 | tf_op jit(solution)/shard_map/all_to_all | solution.py:29
  51.3 3.5 %collective-permute-start.2 = (bf16[128,2048]{1,0:T(8,128)(2,1)}, bf16[128,2048]{1,0:T(8,128)(2,1)S(1)}, u32[]{:S(2)}, u32[]{:S(2)}) collective-permute-start(bf16[128,2048]{1,0:T(8,128)(2,1)} %get-tuple-element.38), channel_id=1, source_target_pairs={{0,16},{8,24},{16,0},{24,8},{1,17},{9,25},{17,1},{25,9},{2,18},{10... | collective-permute-start | bytes 1572872 | tf_op jit(solution)/shard_map/ppermute | solution.py:140
  54.8 2.1 %multiply_reduce_fusion = f32[128]{0:T(128)S(1)} fusion(bf16[128,8192]{1,0:T(8,128)(2,1)} %param.10), kind=kLoop, calls=%fused_computation.1 | loop fusion | flops 3145600 | bytes 2097664 | tf_op jit(solution)/shard_map/reduce_sum | solution.py:267
  56.9 9.6 %collective-permute-done.2.refs_2_ = bf16[128,2048]{1,0:T(8,128)(2,1)S(1)} collective-permute-done((bf16[128,2048]{1,0:T(8,128)(2,1)}, bf16[128,2048]{1,0:T(8,128)(2,1)S(1)}, u32[]{:S(2)}, u32[]{:S(2)}) %collective-permute-start.2) | collective-permute-done | bytes 524320 | tf_op jit(solution)/shard_map/ppermute | solution.py:140
  66.6 4.5 %collective-permute-start.3 = (bf16[4,8,144,128]{3,2,1,0:T(8,128)(2,1)S(1)}, bf16[4,8,144,128]{3,2,1,0:T(8,128)(2,1)S(1)}, u32[]{:S(2)}, u32[]{:S(2)}) collective-permute-start(bf16[4,8,144,128]{3,2,1,0:T(8,128)(2,1)S(1)} %all-to-all-done.1.weights), channel_id=1, source_target_pairs={{0,32},{32,0},{1,33},{33,1},{2,34},{34,2},{3,35},{35,3},{4,36},{36... | collective-permute-start | bytes 3538952 | tf_op jit(solution)/shard_map/ppermute | solution.py:129
  71.2 1.7 %shard_map.114.begun = f32[512,576]{1,0:T(8,128)S(1)} custom-call(s32[2]{0:T(128)S(1)} %pad_add_fusion.place, bf16[4,8,144,128]{3,2,1,0:T(8,128)(2,1)S(1)} %all-to-all-done.1.weights, bf16[128,2048]{1,0:T(8,128)(2,1)S(1)} %get-tuple-element.20.refs_0_, bf16[128,2048]{1,0:T(8,128)(2,1)S(1)} %collective-permute-done.refs_1_, ...), custom_call_target="tpu_custom_call" | custom-call | flops 603979776 | bytes 4194304 | tf_op jit(solution)/shard_map/pallas_call | solution.py:87
  73.6 2.6 %shard_map.115 = bf16[4,128,640]{2,1,0:T(8,128)(2,1)} custom-call(s32[2]{0:T(128)S(1)} %pad_add_fusion.place, bf16[4,8,144,128]{3,2,1,0:T(8,128)(2,1)S(1)} %collective-permute-done.3.weights, f32[512,576]{1,0:T(8,128)S(1)} %shard_map.114.begun, bf16[128,2048]{1,0:T(8,128)(2,1)S(1)} %get-tuple-element.20.refs_0_, ...), custom_call_target="tpu_custom_call" | custom-call | flops 603979776 | bytes 4194304 | tf_op jit(solution)/shard_map/pallas_call | solution.py:87
  76.2 3.5 %all-to-all-start.2 = ((bf16[4,128,640]{2,1,0:T(8,128)(2,1)}), bf16[4,128,640]{2,1,0:T(8,128)(2,1)S(1)}, u32[]{:S(2)}, u32[]{:S(2)}) async-start(bf16[4,128,640]{2,1,0:T(8,128)(2,1)} %shard_map.115), calls=%async_computation.2 | async-start | bytes 1310720 | tf_op jit(solution)/shard_map/all_to_all | solution.py:29
  79.7 10.5 %all-to-all-done.2 = bf16[4,128,640]{2,1,0:T(8,128)(2,1)S(1)} async-done(((bf16[4,128,640]{2,1,0:T(8,128)(2,1)}), bf16[4,128,640]{2,1,0:T(8,128)(2,1)S(1)}, u32[]{:S(2)}, u32[]{:S(2)}) %all-to-all-start.2) | async-done | bytes 655392 | tf_op jit(solution)/shard_map/all_to_all | solution.py:29
  92.2 5.7 %all-to-all-start.3 = ((bf16[8,8,4096]{2,1,0:T(8,128)(2,1)}), bf16[8,8,4096]{2,1,0:T(8,128)(2,1)S(1)}, u32[]{:S(2)}, u32[]{:S(2)}) async-start(bf16[8,8,4096]{2,1,0:T(8,128)(2,1)} %broadcast_in_dim.15), calls=%async_computation.3 | async-start | bytes 1048576 | tf_op jit(solution)/shard_map/all_to_all | solution.py:29
  98.1 1.4 slice.19
  99.7 4.5 %collective-permute-start.6 = (bf16[32,4096]{1,0:T(8,128)(2,1)S(1)}, bf16[32,4096]{1,0:T(8,128)(2,1)S(1)}, u32[]{:S(2)}, u32[]{:S(2)}) collective-permute-start(bf16[32,4096]{1,0:T(8,128)(2,1)S(1)} %reshape.185), channel_id=1, source_target_pairs={{0,24},{8,0},{16,8},{24,16},{1,25},{9,1},{17,9},{25,17},{2,26},{10... | collective-permute-start | bytes 786440 | tf_op jit(solution)/shard_map/ppermute | solution.py:214
  104.1 2.4 %collective-permute-start.5 = (bf16[32,4096]{1,0:T(8,128)(2,1)S(1)}, bf16[32,4096]{1,0:T(8,128)(2,1)S(1)}, u32[]{:S(2)}, u32[]{:S(2)}) collective-permute-start(bf16[32,4096]{1,0:T(8,128)(2,1)S(1)} %reshape.185), channel_id=1, source_target_pairs={{0,16},{8,24},{16,0},{24,8},{1,17},{9,25},{17,1},{25,9},{2,18},{10... | collective-permute-start | bytes 786440 | tf_op jit(solution)/shard_map/ppermute | solution.py:214
  106.5 2.3 %collective-permute-start.4 = (bf16[32,4096]{1,0:T(8,128)(2,1)S(1)}, bf16[32,4096]{1,0:T(8,128)(2,1)S(1)}, u32[]{:S(2)}, u32[]{:S(2)}) collective-permute-start(bf16[32,4096]{1,0:T(8,128)(2,1)S(1)} %reshape.185), channel_id=1, source_target_pairs={{0,8},{8,16},{16,24},{24,0},{1,9},{9,17},{17,25},{25,1},{2,10},{10... | collective-permute-start | bytes 786440 | tf_op jit(solution)/shard_map/ppermute | solution.py:214
  108.8 3.5 %fusion.1 = (f32[4,8,128]{2,1,0:T(8,128)S(1)}, f32[4,128,128,8]{2,1,3,0:T(8,128)}) fusion(f32[4,8,128,128]{2,3,1,0:T(8,128)} %get-tuple-element.43, f32[4,8,128]{2,1,0:T(8,128)S(1)} %copy-done.10, bf16[128,4,128,1]{0,2,3,1:T(8,128)(2,1)S(1)} %bitcast.85, bf16[128,4,8,128]{3,2,1,0:T(8,128)(2,1)S(1)} %bitcast.82), kind=kOutput, calls=%fused_computation.4 | convolution fusion | flops 135786496 | bytes 5406720 | tf_op jit(solution)/shard_map/tjgd,ujd->jgtu/dot_general | solution.py:72
  112.8 2.7 %collective-permute-done.4 = bf16[32,4096]{1,0:T(8,128)(2,1)S(1)} collective-permute-done((bf16[32,4096]{1,0:T(8,128)(2,1)S(1)}, bf16[32,4096]{1,0:T(8,128)(2,1)S(1)}, u32[]{:S(2)}, u32[]{:S(2)}) %collective-permute-start.4) | collective-permute-done | bytes 262176 | tf_op jit(solution)/shard_map/ppermute | solution.py:214
  117.0 15.0 %all-to-all-start.4 = ((f32[8,8,128]{2,1,0:T(8,128)}), f32[8,8,128]{2,1,0:T(8,128)S(1)}, u32[]{:S(2)}, u32[]{:S(2)}) async-start(f32[8,8,128]{2,1,0:T(8,128)} %convolution_bitcast_fusion.2), calls=%async_computation.4 | async-start | bytes 65536 | tf_op jit(solution)/shard_map/all_to_all | solution.py:29
  132.0 2.7 %fusion.6 = bf16[4,128,128]{1,2,0:T(8,128)(2,1)S(1)} fusion(bf16[128,4,8,128]{0,3,2,1:T(8,128)(2,1)S(1)} %bitcast.80, f32[4,128,128,8]{2,1,3,0:T(8,128)} %get-tuple-element.45, f32[4,8,128]{2,1,0:T(8,128)S(1)} %get-tuple-element.44, f32[4,8,128,128]{2,3,1,0:T(8,128)} %get-tuple-element.43, f32[4,8,128]{2,1,0:T(8,128)S(1)} %copy-done.10), kind=kOutput, calls=%fused_computation.14 | convolution fusion | flops 136445952 | bytes 5406720 | tf_op jit(solution)/shard_map/jgtu,tjgd->ujd/dot_general | solution.py:77
  135.5 1.2 all-to-all-done.4
  (60 shorter events, 8.5 us)
Async XLA Ops:
  7.2 38.7 %copy-start = (bf16[512,64]{0,1:T(8,128)(2,1)S(1)}, bf16[512,64]{0,1:T(8,128)(2,1)}, u32[]{:S(2)}) copy-start(bf16[512,64]{0,1:T(8,128)(2,1)} %param.14) | copy-start | bytes 196612
  8.2 1.0 copy-start.1
  9.1 0.7 copy-start.2
  11.2 34.8 %all-to-all-start = ((bf16[8,144,128]{2,1,0:T(8,128)(2,1)}), bf16[8,144,128]{2,1,0:T(8,128)(2,1)S(1)}, u32[]{:S(2)}, u32[]{:S(2)}) async-start(bf16[8,144,128]{2,1,0:T(8,128)(2,1)} %shard_map.113), calls=%async_computation | async-start | bytes 589824 | tf_op jit(solution)/shard_map/all_to_all | solution.py:29
  24.3 73.8 %all-gather.3.cloned.1.call-start = ((), (), s32[]{:S(2)}) async-start(), calls=%async_computation.5 | async-start | bytes 2228224 | tf_op jit(solution)/shard_map/all_gather | solution.py:207
  24.4 9.4 %copy-start.7 = (bf16[2,4096]{1,0:T(2,128)(2,1)S(1)}, bf16[2,4096]{1,0:T(2,128)(2,1)}, u32[]{:S(2)}) copy-start(bf16[2,4096]{1,0:T(2,128)(2,1)} %param.19) | copy-start | bytes 49156
  24.4 10.1 %copy-start.8 = (s32[1,8]{1,0:T(1,128)S(1)}, s32[1,8]{1,0:T(1,128)}, u32[]{:S(2)}) copy-start(s32[1,8]{1,0:T(1,128)} %param.18) | copy-start | bytes 100
  24.4 10.5 %copy-start.3 = (bf16[128,4096]{1,0:T(8,128)(2,1)S(1)}, bf16[128,4096]{1,0:T(8,128)(2,1)}, u32[]{:S(2)}) copy-start(bf16[128,4096]{1,0:T(8,128)(2,1)} %param.15) | copy-start | bytes 3145732
  27.2 18.8 %collective-permute-start = (bf16[128,2048]{1,0:T(8,128)(2,1)}, bf16[128,2048]{1,0:T(8,128)(2,1)S(1)}, u32[]{:S(2)}, u32[]{:S(2)}) collective-permute-start(bf16[128,2048]{1,0:T(8,128)(2,1)} %get-tuple-element.40), channel_id=1, source_target_pairs={{0,8},{8,16},{16,24},{24,0},{1,9},{9,17},{17,25},{25,1},{2,10},{10... | collective-permute-start | bytes 1572872 | tf_op jit(solution)/shard_map/ppermute | solution.py:140
  30.4 15.6 %collective-permute-start.1 = (bf16[128,2048]{1,0:T(8,128)(2,1)S(1)}, bf16[128,2048]{1,0:T(8,128)(2,1)S(1)}, u32[]{:S(2)}, u32[]{:S(2)}) collective-permute-start(bf16[128,2048]{1,0:T(8,128)(2,1)S(1)} %get-tuple-element.39), channel_id=1, source_target_pairs={{0,24},{8,0},{16,8},{24,16},{1,25},{9,1},{17,9},{25,17},{2,26},{10... | collective-permute-start | bytes 1572872 | tf_op jit(solution)/shard_map/ppermute | solution.py:140
  36.2 4.1 %copy-start.4 = (bf16[128,4096]{0,1:T(8,128)(2,1)S(1)}, bf16[128,4096]{0,1:T(8,128)(2,1)}, u32[]{:S(2)}) copy-start(bf16[128,4096]{0,1:T(8,128)(2,1)} %copy.72) | copy-start | bytes 3145732
  43.4 2.5 %copy-start.9 = (f32[4,8,128]{2,1,0:T(8,128)}, f32[4,8,128]{2,1,0:T(8,128)S(1)}, u32[]{:S(2)}) copy-start(f32[4,8,128]{2,1,0:T(8,128)S(1)} %get-tuple-element.42) | copy-start | bytes 49156
  47.3 19.3 %all-to-all-start.1 = ((bf16[4,8,144,128]{3,2,1,0:T(8,128)(2,1)}), bf16[4,8,144,128]{3,2,1,0:T(8,128)(2,1)S(1)}, u32[]{:S(2)}, u32[]{:S(2)}) async-start(bf16[4,8,144,128]{3,2,1,0:T(8,128)(2,1)} %broadcast_in_dim.14), calls=%async_computation.1 | async-start | bytes 2359296 | tf_op jit(solution)/shard_map/all_to_all | solution.py:29
  51.3 15.3 %collective-permute-start.2 = (bf16[128,2048]{1,0:T(8,128)(2,1)}, bf16[128,2048]{1,0:T(8,128)(2,1)S(1)}, u32[]{:S(2)}, u32[]{:S(2)}) collective-permute-start(bf16[128,2048]{1,0:T(8,128)(2,1)} %get-tuple-element.38), channel_id=1, source_target_pairs={{0,16},{8,24},{16,0},{24,8},{1,17},{9,25},{17,1},{25,9},{2,18},{10... | collective-permute-start | bytes 1572872 | tf_op jit(solution)/shard_map/ppermute | solution.py:140
  66.6 7.0 %collective-permute-start.3 = (bf16[4,8,144,128]{3,2,1,0:T(8,128)(2,1)S(1)}, bf16[4,8,144,128]{3,2,1,0:T(8,128)(2,1)S(1)}, u32[]{:S(2)}, u32[]{:S(2)}) collective-permute-start(bf16[4,8,144,128]{3,2,1,0:T(8,128)(2,1)S(1)} %all-to-all-done.1.weights), channel_id=1, source_target_pairs={{0,32},{32,0},{1,33},{33,1},{2,34},{34,2},{3,35},{35,3},{4,36},{36... | collective-permute-start | bytes 3538952 | tf_op jit(solution)/shard_map/ppermute | solution.py:129
  76.2 14.1 %all-to-all-start.2 = ((bf16[4,128,640]{2,1,0:T(8,128)(2,1)}), bf16[4,128,640]{2,1,0:T(8,128)(2,1)S(1)}, u32[]{:S(2)}, u32[]{:S(2)}) async-start(bf16[4,128,640]{2,1,0:T(8,128)(2,1)} %shard_map.115), calls=%async_computation.2 | async-start | bytes 1310720 | tf_op jit(solution)/shard_map/all_to_all | solution.py:29
  90.3 18.5 %copy-start.6 = (bf16[16,8,32,128]{3,2,1,0:T(8,128)(2,1)S(1)}, bf16[16,8,32,128]{3,2,1,0:T(8,128)(2,1)}, u32[]{:S(2)}) copy-start(bf16[16,8,32,128]{3,2,1,0:T(8,128)(2,1)} %copy.73) | copy-start | bytes 3145732
  90.3 18.5 %copy-start.10 = (f32[4,8,128]{2,1,0:T(8,128)S(1)}, f32[4,8,128]{2,1,0:T(8,128)}, u32[]{:S(2)}) copy-start(f32[4,8,128]{2,1,0:T(8,128)} %copy-done.9) | copy-start | bytes 49156
  92.2 23.5 %all-to-all-start.3 = ((bf16[8,8,4096]{2,1,0:T(8,128)(2,1)}), bf16[8,8,4096]{2,1,0:T(8,128)(2,1)S(1)}, u32[]{:S(2)}, u32[]{:S(2)}) async-start(bf16[8,8,4096]{2,1,0:T(8,128)(2,1)} %broadcast_in_dim.15), calls=%async_computation.3 | async-start | bytes 1048576 | tf_op jit(solution)/shard_map/all_to_all | solution.py:29
  99.7 12.7 %collective-permute-start.6 = (bf16[32,4096]{1,0:T(8,128)(2,1)S(1)}, bf16[32,4096]{1,0:T(8,128)(2,1)S(1)}, u32[]{:S(2)}, u32[]{:S(2)}) collective-permute-start(bf16[32,4096]{1,0:T(8,128)(2,1)S(1)} %reshape.185), channel_id=1, source_target_pairs={{0,24},{8,0},{16,8},{24,16},{1,25},{9,1},{17,9},{25,17},{2,26},{10... | collective-permute-start | bytes 786440 | tf_op jit(solution)/shard_map/ppermute | solution.py:214
  104.1 8.7 %collective-permute-start.5 = (bf16[32,4096]{1,0:T(8,128)(2,1)S(1)}, bf16[32,4096]{1,0:T(8,128)(2,1)S(1)}, u32[]{:S(2)}, u32[]{:S(2)}) collective-permute-start(bf16[32,4096]{1,0:T(8,128)(2,1)S(1)} %reshape.185), channel_id=1, source_target_pairs={{0,16},{8,24},{16,0},{24,8},{1,17},{9,25},{17,1},{25,9},{2,18},{10... | collective-permute-start | bytes 786440 | tf_op jit(solution)/shard_map/ppermute | solution.py:214
  106.5 9.0 %collective-permute-start.4 = (bf16[32,4096]{1,0:T(8,128)(2,1)S(1)}, bf16[32,4096]{1,0:T(8,128)(2,1)S(1)}, u32[]{:S(2)}, u32[]{:S(2)}) collective-permute-start(bf16[32,4096]{1,0:T(8,128)(2,1)S(1)} %reshape.185), channel_id=1, source_target_pairs={{0,8},{8,16},{16,24},{24,0},{1,9},{9,17},{17,25},{25,1},{2,10},{10... | collective-permute-start | bytes 786440 | tf_op jit(solution)/shard_map/ppermute | solution.py:214
  112.3 19.6 %copy-start.5 = (bf16[128,4096]{0,1:T(8,128)(2,1)S(1)}, bf16[128,4096]{0,1:T(8,128)(2,1)}, u32[]{:S(2)}) copy-start(bf16[128,4096]{0,1:T(8,128)(2,1)} %copy.72) | copy-start | bytes 3145732
  117.0 19.7 %all-to-all-start.4 = ((f32[8,8,128]{2,1,0:T(8,128)}), f32[8,8,128]{2,1,0:T(8,128)S(1)}, u32[]{:S(2)}, u32[]{:S(2)}) async-start(f32[8,8,128]{2,1,0:T(8,128)} %convolution_bitcast_fusion.2), calls=%async_computation.4 | async-start | bytes 65536 | tf_op jit(solution)/shard_map/all_to_all | solution.py:29
Sparse Core Ops, SparseCore 0:
  34.7 63.4 all-gather.2

commit v3 on v2

v3 whole, which is shorter than its diff:
```python
import itertools
import math

import jax
import jax.numpy as jnp
from jax import lax
from jax.experimental import pallas as pl
from jax.experimental.pallas import tpu as pltpu
from jax.sharding import Mesh
from jax.sharding import PartitionSpec as P

HD = 128
GROUP = 8
KVH = 4
RANK = 64
LANES = 128

epsilon = 1e-05

AXES = ("zh", "x", "c", "y", "zl")
SIZES = (2, 4, 2, 4, 8)
XS = 4


def width(axes):
    return math.prod(lax.axis_size(a) for a in axes)


def exchange(blocks, axes):
    return lax.all_to_all(blocks, axes, 0, 0, tiled=False)


def spread(block, axes):
    return exchange(jnp.broadcast_to(block[None], (width(axes),) + block.shape), axes)


def segments(lengths, count):
    bounds = jnp.cumsum(lengths)
    places = jnp.arange(count, dtype=jnp.int32)
    return jnp.sum((places[:, None] >= bounds[None, :]).astype(jnp.int32), axis=1)


def spec(space):
    return pl.BlockSpec(memory_space=space)


def local_kernel(body, out_shape, scratch=(), flops=0, moved=0):
    def call(place, *arrays):
        return pl.pallas_call(
            body,
            out_shape=out_shape,
            in_specs=[spec(pltpu.SMEM)] + [spec(pltpu.VMEM)] * len(arrays),
            out_specs=jax.tree.map(lambda _: spec(pltpu.VMEM), out_shape),
            scratch_shapes=scratch,
            compiler_params=pltpu.CompilerParams(vmem_limit_bytes=16 * 1024 * 1024),
            cost_estimate=pl.CostEstimate(flops=flops, bytes_accessed=moved, transcendentals=0),
        )(place, *arrays)

    return call


def segment_of(lengths, index):
    found, bound = jnp.zeros_like(index), 0
    for e in range(lengths.shape[1]):
        bound = bound + lengths[0, e]
        found = found + (index >= bound).astype(jnp.int32)
    return found


def group_rows(array, j):
    heads = [array[:, (j * GROUP + g) * HD : (j * GROUP + g + 1) * HD] for g in range(GROUP)]
    return jnp.concatenate(heads, axis=0)


def probs_kernel(lengths, queries, keys, upstream, basis, probs, right):
    count = queries.shape[0]
    row = lax.broadcasted_iota(jnp.int32, (count, count), 0)
    column = lax.broadcasted_iota(jnp.int32, (count, count), 1)
    allowed = (segment_of(lengths, row) == segment_of(lengths, column)) & (row <= column)
    fence = jnp.where(allowed, 0.0, -1e30).astype(jnp.float32)
    fence = jnp.concatenate([fence] * GROUP, axis=1)
    scale = 1.0 / math.sqrt(HD)
    grads = []
    for j in range(KVH):
        logits = lax.dot_general(
            keys[:, j * HD : (j + 1) * HD],
            group_rows(queries, j),
            (((1,), (1,)), ((), ())),
            preferred_element_type=jnp.float32,
        )
        logits = jnp.where(fence == 0.0, logits * scale, fence)
        expo = jnp.exp(logits - jnp.max(logits, axis=0, keepdims=True))
        prob = expo * (1.0 / jnp.sum(expo, axis=0, keepdims=True))
        probs[j] = prob
        grad = jnp.dot(
            prob.astype(jnp.bfloat16), group_rows(upstream, j), preferred_element_type=jnp.float32
        )
        grads.append(grad.astype(jnp.bfloat16))
    right[...] = lax.dot_general(
        jnp.concatenate(grads, axis=1),
        basis[...],
        (((1,), (1,)), ((), ())),
        preferred_element_type=jnp.float32,
    )


def keys_kernel(lengths, queries, probs, values, upstream, key_grad):
    scale = 1.0 / math.sqrt(HD)
    for j in range(KVH):
        columns = slice(j * HD, (j + 1) * HD)
        prob_grad = lax.dot_general(
            values[:, columns],
            group_rows(upstream, j),
            (((1,), (1,)), ((), ())),
            preferred_element_type=jnp.float32,
        )
        prob = probs[j]
        mean = jnp.sum(prob * prob_grad, axis=0, keepdims=True)
        logit_grad = (prob * (prob_grad - mean)).astype(jnp.bfloat16)
        grad = jnp.dot(logit_grad, group_rows(queries, j), preferred_element_type=jnp.float32)
        key_grad[:, columns] = (grad * scale).astype(jnp.bfloat16)


def attend_probs(queries, keys, upstream, lengths, basis):
    count = queries.shape[0]
    out = (
        jax.ShapeDtypeStruct((KVH, count, GROUP * count), jnp.float32),
        jax.ShapeDtypeStruct((count, RANK), jnp.float32),
    )
    cost = dict(flops=4 * KVH * GROUP * count * count * HD, moved=5 << 20)
    return local_kernel(probs_kernel, out, **cost)(lengths, queries, keys, upstream, basis.T)


def attend_keys(queries, probs, values, upstream, lengths):
    out = jax.ShapeDtypeStruct(values.shape, jnp.bfloat16)
    cost = dict(flops=4 * KVH * GROUP * HD * values.shape[0] ** 2, moved=5 << 20)
    return local_kernel(keys_kernel, out, **cost)(lengths, queries, probs, values, upstream)


def first_kernel(place, gain, values, basis, queries, out, turned):
    c, x, block = place[0], place[1], place[2]
    rows = pl.ds(pl.multiple_of(c * LANES, LANES), LANES)
    mine = lax.broadcasted_iota(jnp.int32, gain.shape, 0) == block
    factor = jnp.sum(jnp.where(mine, gain[...].astype(jnp.float32), 0.0), axis=0, keepdims=True)
    head = values[rows, pl.ds(pl.multiple_of(x * HD, HD), HD)].astype(jnp.float32)
    turned[...] = basis[:, rows].astype(jnp.float32)
    share = RANK // XS
    some = turned[pl.ds(pl.multiple_of(x * share, share), share), :]
    piece = jnp.concatenate([head.T, some], axis=0) * factor
    length = queries.shape[1] // LANES
    wide = queries[...].astype(jnp.float32)
    cut = [wide[:, k * LANES : (k + 1) * LANES] for k in range(length)]
    both = jnp.concatenate([piece] + cut, axis=0).astype(out.dtype)
    out[...] = jnp.broadcast_to(both[None], out.shape)


def gather_along_z(norm_gain, value_weight, input_basis, query_grads):
    c, x = lax.axis_index("c"), lax.axis_index("x")
    zs = lax.axis_size("zl")
    shard = lax.axis_index("y") * zs + lax.axis_index("zl")
    place = jnp.stack([c, x, shard * lax.axis_size("c") + c]).astype(jnp.int32)
    columns = HD + RANK // lax.axis_size("x")
    rows, length = query_grads.shape
    sent = local_kernel(
        first_kernel,
        jax.ShapeDtypeStruct((zs, columns + rows * length // LANES, LANES), jnp.bfloat16),
        (pltpu.VMEM((RANK, LANES), jnp.float32),),
        moved=1 << 20,
    )(place, norm_gain.reshape(-1, LANES), value_weight, input_basis.T, query_grads)
    came = exchange(sent, ("zl",))
    queries = came[:, columns:].reshape(zs, length // LANES, rows, LANES)
    return came[:, :columns], queries.transpose(0, 2, 1, 3).reshape(zs * rows, length)


def swapped(block):
    return lax.ppermute(block, "c", [(0, 1), (1, 0)])


def share_tokens(tokens):
    ys = lax.axis_size("y")
    features = tokens.shape[1] // ys
    blocks = []
    for s in range(ys):
        target = lax.rem(lax.axis_index("y") + s, ys)
        block = lax.dynamic_slice_in_dim(tokens, target * features, features, 1)
        if s:
            block = lax.ppermute(block, "y", [(i, (i + s) % ys) for i in range(ys)])
        blocks.append(block)
    return blocks


def lay_out(weights, half, whole):
    xs, zs, width_, depth = weights.shape
    share = width_ - HD
    for z in range(zs):
        features = pl.ds(pl.multiple_of((2 * z + half) * depth, depth), depth)
        for x in range(xs):
            whole[x * HD : (x + 1) * HD, features] = weights[x, z, :HD, :]
            begin = xs * HD + x * share
            whole[begin : begin + share, features] = weights[x, z, HD:, :]


def product_kernel(place, own, partners, *refs):
    *blocks, out, whole = refs
    y, c = place[0], place[1]
    count, wide, ys = blocks[0].shape[0], KVH * HD, len(blocks)
    lay_out(own, c, whole)
    lay_out(partners, 1 - c, whole)
    total = lax.dot_general(
        jnp.concatenate([block[...] for block in blocks], axis=0),
        whole[...],
        (((1,), (1,)), ((), ())),
        preferred_element_type=jnp.float32,
    )
    left = total[:, wide:]
    high = left.astype(jnp.bfloat16)
    low = (left - high.astype(jnp.float32)).astype(jnp.bfloat16)
    sent = jnp.concatenate([total[:, :wide].astype(jnp.bfloat16), high, low], axis=1)
    for distance in range(ys):
        out[lax.rem(y - distance + ys, ys)] = sent[distance * count : (distance + 1) * count]


def project(blocks, weights):
    ys, (count, features) = len(blocks), blocks[0].shape
    xs, _, width_, _ = weights.shape
    columns = xs * width_
    place = jnp.stack([lax.axis_index("y"), lax.axis_index("c")]).astype(jnp.int32)
    return local_kernel(
        product_kernel,
        jax.ShapeDtypeStruct((ys, count, columns + RANK), jnp.bfloat16),
        (pltpu.VMEM((columns, features), jnp.bfloat16),),
        flops=2 * ys * count * columns * features,
        moved=6 << 20,
    )(place, weights, swapped(weights), *blocks)


def pair(block, axis, bit):
    size = lax.axis_size(axis)
    other = lax.ppermute(block, axis, [(i, i ^ bit) for i in range(size)])
    return jnp.concatenate([block, other], axis=0)


def bits(axis):
    return [1 << k for k in range(lax.axis_size(axis).bit_length() - 1)]


def query_steps():
    return [("zh", b) for b in bits("zh")] + [("y", b) for b in bits("y")]


def query_order(rows):
    sizes = [lax.axis_size(a) for a in ("zh", "y", "zl")]
    n = jnp.arange(math.prod(sizes) * rows, dtype=jnp.int32)
    left, row = n // rows, n % rows
    where = {}
    for axis, size in zip(("zl", "y", "zh"), sizes[::-1]):
        where[axis] = left % size
        left = left // size
    k, weight = where["zl"] * rows + row, rows * sizes[2]
    for axis in ("y", "zh"):
        where[axis] = where[axis] ^ lax.axis_index(axis).astype(jnp.int32)
    for axis, bit in query_steps():
        k = k + jnp.where((where[axis] & bit) != 0, weight, 0)
        weight = weight * 2
    return (n[:, None] == k[None, :]).astype(jnp.float32)


def score(others, some_queries, pick):
    xs, cs, zhs = lax.axis_size("x"), lax.axis_size("c"), lax.axis_size("zh")
    count = others.shape[1]
    block = lax.dot_general(
        others.reshape(xs * cs * count, -1),
        some_queries,
        (((1,), (1,)), ((), ())),
        preferred_element_type=jnp.float32,
    )
    block = jnp.dot(block, pick, precision=lax.Precision.HIGHEST)
    came = exchange(block.reshape(xs * cs, count, -1), ("x", "c"))
    came = came.reshape(xs, cs, count, zhs, -1)
    return came.transpose(2, 3, 0, 1, 4).reshape(count, -1)


def on_device(
    tokens,
    norm_gain,
    value_weight,
    input_basis,
    output_basis,
    rotated_queries,
    rotated_keys,
    upstream_grad,
    example_lengths,
    query_grads,
):
    steps = iter(query_steps())
    along_z, gathered = gather_along_z(norm_gain, value_weight, input_basis, query_grads)
    blocks = share_tokens(tokens)
    along_z, gathered, blocks[1], blocks[-1] = lax.optimization_barrier(
        (along_z, gathered, blocks[1], blocks[-1])
    )

    weights = spread(along_z, ("x",))
    for step in itertools.islice(steps, 1):
        gathered = pair(gathered, *step)
    activ = tokens.astype(jnp.float32)
    row_scale = lax.rsqrt(jnp.mean(activ * activ, axis=1, keepdims=True) + epsilon)
    weights, gathered, *blocks = lax.optimization_barrier((weights, gathered, *blocks))

    sent = project(blocks, weights)
    sent, rotated_queries, upstream_grad = lax.optimization_barrier(
        (sent, rotated_queries, upstream_grad)
    )
    came = exchange(sent, ("y",))
    probs, right = attend_probs(
        rotated_queries, rotated_keys, upstream_grad, example_lengths, output_basis
    )
    for step in itertools.islice(steps, 1):
        gathered = pair(gathered, *step)
    pick = query_order(query_grads.shape[0])
    came, gathered, pick, right, row_scale = lax.optimization_barrier(
        (came, gathered, pick, right, row_scale)
    )
    total = jnp.sum(came.astype(jnp.float32), axis=0)
    wide = KVH * HD
    values = (total[:, :wide] * row_scale).astype(jnp.bfloat16)
    left = (total[:, wide : wide + RANK] + total[:, wide + RANK :]) * row_scale

    examples = example_lengths.shape[1]
    segment = segments(example_lengths[0], tokens.shape[0])
    onehot = (segment[:, None] == jnp.arange(examples, dtype=jnp.int32)[None, :]).astype(jnp.float32)
    per_example = jnp.einsum("te,ti,tj->eij", onehot, left, right, precision=lax.Precision.HIGHEST)
    train_grads = per_example.reshape(examples, -1).astype(jnp.bfloat16)
    others = spread(train_grads, ("x", "c"))
    for step in steps:
        gathered = pair(gathered, *step)
    key_grad = attend_keys(rotated_queries, probs, values, upstream_grad, example_lengths)
    others, gathered, key_grad = lax.optimization_barrier((others, gathered, key_grad))
    return (key_grad, score(others, gathered, pick))


def solution(mesh):
    fine = Mesh(mesh.devices.reshape(SIZES), AXES)
    rows = P(AXES, None)
    return jax.shard_map(
        on_device,
        mesh=fine,
        in_specs=(
            rows,
            P(),
            P(("y", "zl"), None),
            P(("y", "zl"), None),
            P(),
            rows,
            rows,
            rows,
            rows,
            rows,
        ),
        out_specs=(rows, rows),
        check_vma=False,
    )
```

time: 145 us -> 132 us (0.910)
  between operations: 14.4 us -> 0.96 us
  matrix products: 13.6 us -> 1.06 us
  blocking collectives: 0 us -> 8.48 us
  Pallas kernels: 5.72 us -> 10.2 us
  local copies, waits for them, and re-layouts: 17.1 us -> 12.7 us
  other arithmetic: 3 us -> 6.34 us
    all_to_all x5 -> x4, starting transfers between devices: 41.3 us -> 27.5 us  [exchange(): return lax.all_to_all(blocks, axes, 0, 0, tiled=False)]
    dot_general x4 -> x0, matrix products: 8.85 us -> none  [the longest x1 3.5 us: attend_keys(): jnp.einsum('tjgd,ujd->jgtu', grad_heads, value_heads, preferred_element_t...]
    ppermute x1, starting transfers between devices: 4.55 us -> 13.1 us  [swapped(): return lax.ppermute(block, 'c', [(0, 1), (1, 0)])]
    all_to_all x0 -> x1, blocking collectives: none -> 8.48 us  [exchange(): return lax.all_to_all(blocks, axes, 0, 0, tiled=False)]
    all_to_all x5 -> x4, waiting for transfers between devices: 11.8 us -> 18 us  [exchange(): return lax.all_to_all(blocks, axes, 0, 0, tiled=False)]
    pallas_call x3 -> x4, Pallas kernels: 5.72 us -> 10.2 us  [call(): pl.pallas_call(body, out_shape=out_shape, in_specs=[spec(pltpu.SMEM)] + [...]
    ppermute x3, waiting for transfers between devices: 9.65 us -> 5.27 us  [share_tokens(): block = lax.ppermute(block, 'y', [(i, (i + s) % ys) for i in range(ys)])]
    ppermute x3, starting transfers between devices: 9.14 us -> 13.4 us  [pair(): other = lax.ppermute(block, axis, [(i, i ^ bit) for i in range(size)])]
  transfers between devices with their start and end apart: 13 -> 11, of which waited for: 7 -> 7; matrix products, arithmetic and copies ran while one was open for 20% -> 8% of each run, Pallas kernels for 3% -> 7%
where the time goes in v3:
time: 132 us; the launch traced here: 131 us
  starting transfers between devices  65.1 us (49%)
  waiting for transfers between devices  26.6 us (20%)
  local copies, waits for them, and re-layouts  12.7 us (10%)
  Pallas kernels  10.2 us (8%)
  blocking collectives  8.48 us (6%)
  other arithmetic  6.34 us (5%)
    all_to_all x4, starting transfers between devices, exchange(): return lax.all_to_all(blocks, axes, 0, 0, tiled=False)  27.5 us
    all_to_all x4, waiting for transfers between devices, exchange(): return lax.all_to_all(blocks, axes, 0, 0, tiled=False)  18 us
    ppermute x3, starting transfers between devices, pair(): other = lax.ppermute(block, axis, [(i, i ^ bit) for i in range(size)])  13.4 us
    ppermute x1, starting transfers between devices, swapped(): return lax.ppermute(block, 'c', [(0, 1), (1, 0)])  13.1 us
    ppermute x3, starting transfers between devices, share_tokens(): block = lax.ppermute(block, 'y', [(i, (i + s) % ys) for i in range(ys)])  11.1 us
    pallas_call x4, Pallas kernels, call(): pl.pallas_call(body, out_shape=out_shape, in_specs=[spec(pltpu.SMEM)] + [...  10.2 us
    all_to_all x1, blocking collectives, exchange(): return lax.all_to_all(blocks, axes, 0, 0, tiled=False)  8.48 us
    unnamed x37, local copies, waits for them, and re-layouts  6.95 us
  transfers between devices with their start and end apart: 11, of which 7 were waited for; matrix products, arithmetic and copies ran while one was open for 8% of the time, Pallas kernels for 7%

profile of v3, /device:TPU:1, one launch (start us, length us, event | category | flops | bytes accessed | tf_op | source)
XLA Modules:
  0.0 131.4 jit_solution(9130983606041047143)
XLA Ops:
  0.7 0.9 copy-done.8
  3.9 1.4 %shard_map.113 = bf16[8,208,128]{2,1,0:T(8,128)(2,1)} custom-call(s32[3]{0:T(128)S(1)} %pad_add_fusion.1.place, bf16[64,128]{1,0:T(8,128)(2,1)S(1)} %bitcast.37, bf16[256,512]{1,0:T(8,128)(2,1)S(1)} %copy-done.8, bf16[64,256]{1,0:T(8,128)(2,1)S(1)} %bitcast.36, bf16[2,4096]{1,0:T(2,128)(2,1)S(1)} %copy-done.13), custom_call_target="tpu_custom_call" | custom-call | bytes 1048576 | tf_op jit(solution)/shard_map/pallas_call | solution.py:49
  5.3 13.1 %all-to-all-start = ((bf16[8,208,128]{2,1,0:T(8,128)(2,1)}), bf16[8,208,128]{2,1,0:T(8,128)(2,1)S(1)}, u32[]{:S(2)}, u32[]{:S(2)}) async-start(bf16[8,208,128]{2,1,0:T(8,128)(2,1)} %shard_map.113), calls=%async_computation | async-start | bytes 851968 | tf_op jit(solution)/shard_map/all_to_all | solution.py:30
  18.4 2.5 %constant_dynamic-slice_fusion = (bf16[128,2048]{1,0:T(8,128)(2,1)S(1)}, bf16[128,2048]{1,0:T(8,128)(2,1)S(1)}, bf16[128,2048]{1,0:T(8,128)(2,1)S(1)}, bf16[128,2048]{1,0:T(8,128)(2,1)}) fusion(bf16[128,8192]{1,0:T(8,128)(2,1)} %param.10, s32[]{:T(128)S(6)} %select_n.101, s32[]{:T(128)S(6)} %select_n.100, s32[]{:T(128)S(6)} %select_n.99, s32[]{:T(128)S(6)} %select_n.98), kind=kLoop, calls=%fused_computation.47 | loop fusion | bytes 4194320 | tf_op jit(solution)/shard_map/dynamic_slice | solution.py:185
  20.9 3.2 %collective-permute-start = (bf16[128,2048]{1,0:T(8,128)(2,1)}, bf16[128,2048]{1,0:T(8,128)(2,1)S(1)}, u32[]{:S(2)}, u32[]{:S(2)}) collective-permute-start(bf16[128,2048]{1,0:T(8,128)(2,1)} %get-tuple-element.51), channel_id=1, source_target_pairs={{0,8},{8,16},{16,24},{24,0},{1,9},{9,17},{17,25},{25,1},{2,10},{10... | collective-permute-start | bytes 1572872 | tf_op jit(solution)/shard_map/ppermute | solution.py:187
  24.1 3.4 %collective-permute-start.1 = (bf16[128,2048]{1,0:T(8,128)(2,1)S(1)}, bf16[128,2048]{1,0:T(8,128)(2,1)S(1)}, u32[]{:S(2)}, u32[]{:S(2)}) collective-permute-start(bf16[128,2048]{1,0:T(8,128)(2,1)S(1)} %get-tuple-element.50), channel_id=1, source_target_pairs={{0,24},{8,0},{16,8},{24,16},{1,25},{9,1},{17,9},{25,17},{2,26},{10... | collective-permute-start | bytes 1572872 | tf_op jit(solution)/shard_map/ppermute | solution.py:187
  27.4 9.2 %all-to-all-done = bf16[8,208,128]{2,1,0:T(8,128)(2,1)S(1)} async-done(((bf16[8,208,128]{2,1,0:T(8,128)(2,1)}), bf16[8,208,128]{2,1,0:T(8,128)(2,1)S(1)}, u32[]{:S(2)}, u32[]{:S(2)}) %all-to-all-start) | async-done | bytes 426016 | tf_op jit(solution)/shard_map/all_to_all | solution.py:30
  36.8 1.3 %collective-permute-done.1.refs_3_ = bf16[128,2048]{1,0:T(8,128)(2,1)S(1)} collective-permute-done((bf16[128,2048]{1,0:T(8,128)(2,1)S(1)}, bf16[128,2048]{1,0:T(8,128)(2,1)S(1)}, u32[]{:S(2)}, u32[]{:S(2)}) %collective-permute-start.1) | collective-permute-done | bytes 524320 | tf_op jit(solution)/shard_map/ppermute | solution.py:187
  38.1 1.2 broadcast_in_dim.18
  39.4 4.0 %all-to-all-start.1 = ((bf16[4,8,144,128]{3,2,1,0:T(8,128)(2,1)}), bf16[4,8,144,128]{3,2,1,0:T(8,128)(2,1)S(1)}, u32[]{:S(2)}, u32[]{:S(2)}) async-start(bf16[4,8,144,128]{3,2,1,0:T(8,128)(2,1)} %broadcast_in_dim.18), calls=%async_computation.1 | async-start | bytes 2359296 | tf_op jit(solution)/shard_map/all_to_all | solution.py:30
  43.4 7.9 %collective-permute-start.2 = (bf16[16,4096]{1,0:T(8,128)(2,1)S(1)}, bf16[16,4096]{1,0:T(8,128)(2,1)S(1)}, u32[]{:S(2)}, u32[]{:S(2)}) collective-permute-start(bf16[16,4096]{1,0:T(8,128)(2,1)S(1)} %bitcast.41), channel_id=1, source_target_pairs={{0,256},{256,0},{1,257},{257,1},{2,258},{258,2},{3,259},{259,3},{4... | collective-permute-start | bytes 393224 | tf_op jit(solution)/shard_map/ppermute | solution.py:239
  51.3 4.5 %collective-permute-start.3 = (bf16[128,2048]{1,0:T(8,128)(2,1)S(1)}, bf16[128,2048]{1,0:T(8,128)(2,1)S(1)}, u32[]{:S(2)}, u32[]{:S(2)}) collective-permute-start(bf16[128,2048]{1,0:T(8,128)(2,1)S(1)} %get-tuple-element.48), channel_id=1, source_target_pairs={{0,16},{8,24},{16,0},{24,8},{1,17},{9,25},{17,1},{25,9},{2,18},{10... | collective-permute-start | bytes 1572872 | tf_op jit(solution)/shard_map/ppermute | solution.py:187
  55.8 2.2 %collective-permute-done.2 = bf16[16,4096]{1,0:T(8,128)(2,1)S(1)} collective-permute-done((bf16[16,4096]{1,0:T(8,128)(2,1)S(1)}, bf16[16,4096]{1,0:T(8,128)(2,1)S(1)}, u32[]{:S(2)}, u32[]{:S(2)}) %collective-permute-start.2) | collective-permute-done | bytes 131104 | tf_op jit(solution)/shard_map/ppermute | solution.py:239
  58.8 3.9 %collective-permute-done.3.refs_2_ = bf16[128,2048]{1,0:T(8,128)(2,1)S(1)} collective-permute-done((bf16[128,2048]{1,0:T(8,128)(2,1)S(1)}, bf16[128,2048]{1,0:T(8,128)(2,1)S(1)}, u32[]{:S(2)}, u32[]{:S(2)}) %collective-permute-start.3) | collective-permute-done | bytes 524320 | tf_op jit(solution)/shard_map/ppermute | solution.py:187
  63.5 13.1 %collective-permute-start.4 = (bf16[4,8,144,128]{3,2,1,0:T(8,128)(2,1)S(1)}, bf16[4,8,144,128]{3,2,1,0:T(8,128)(2,1)S(1)}, u32[]{:S(2)}, u32[]{:S(2)}) collective-permute-start(bf16[4,8,144,128]{3,2,1,0:T(8,128)(2,1)S(1)} %all-to-all-done.1.own), channel_id=1, source_target_pairs={{0,32},{32,0},{1,33},{33,1},{2,34},{34,2},{3,35},{35,3},{4,36},{36... | collective-permute-start | bytes 3538952 | tf_op jit(solution)/shard_map/ppermute | solution.py:176
  77.7 2.1 %multiply_reduce_fusion = f32[128]{0:T(128)S(1)} fusion(bf16[128,8192]{1,0:T(8,128)(2,1)} %param.10), kind=kLoop, calls=%fused_computation | loop fusion | flops 3145600 | bytes 2097664 | tf_op jit(solution)/shard_map/reduce_sum | solution.py:306
  79.8 3.2 %collective-permute-start.5 = (bf16[32,4096]{1,0:T(8,128)(2,1)}, bf16[32,4096]{1,0:T(8,128)(2,1)}, u32[]{:S(2)}, u32[]{:S(2)}) collective-permute-start(bf16[32,4096]{1,0:T(8,128)(2,1)} %pad_maximum_fusion.2), channel_id=1, source_target_pairs={{0,8},{8,0},{16,24},{24,16},{1,9},{9,1},{17,25},{25,17},{2,10},{10... | collective-permute-start | bytes 786440 | tf_op jit(solution)/shard_map/ppermute | solution.py:239
  83.0 4.0 %shard_map.114 = bf16[4,128,640]{2,1,0:T(8,128)(2,1)} custom-call(s32[2]{0:T(128)S(1)} %pad_add_fusion.place, bf16[4,8,144,128]{3,2,1,0:T(8,128)(2,1)S(1)} %all-to-all-done.1.own, bf16[4,8,144,128]{3,2,1,0:T(8,128)(2,1)S(1)} %collective-permute-done.4.partners, bf16[128,2048]{1,0:T(8,128)(2,1)S(1)} %get-tuple-element.30.refs_0_, ...), custom_call_target="tpu_custom_call" | custom-call | flops 1207959552 | bytes 6291456 | tf_op jit(solution)/shard_map/pallas_call | solution.py:49
  87.1 4.0 %all-to-all-start.2 = ((bf16[4,128,640]{2,1,0:T(8,128)(2,1)}), bf16[4,128,640]{2,1,0:T(8,128)(2,1)S(1)}, u32[]{:S(2)}, u32[]{:S(2)}) async-start(bf16[4,128,640]{2,1,0:T(8,128)(2,1)} %shard_map.114), calls=%async_computation.2 | async-start | bytes 1310720 | tf_op jit(solution)/shard_map/all_to_all | solution.py:30
  91.1 1.1 pad_maximum_fusion.1
  92.2 2.3 %shard_map.115 = (f32[4,128,1024]{2,1,0:T(8,128)S(1)}, f32[128,64]{1,0:T(8,128)S(1)}) custom-call(s32[1,8]{1,0:T(1,128)S(1)} %copy-done.14, bf16[128,4096]{1,0:T(8,128)(2,1)S(1)} %copy-done, bf16[128,512]{1,0:T(8,128)(2,1)S(1)} %copy-done.9, bf16[128,4096]{1,0:T(8,128)(2,1)S(1)} %copy-done.1, bf16[64,512]{1,0:T(8,128)(2,1)S(1)} %bitcast.35), custom_call_target="tpu_custom_call" | custom-call | flops 268435456 | bytes 5242880 | tf_op jit(solution)/shard_map/pallas_call | solution.py:49
  94.5 1.3 %copy-done.2 = f32[4,128,1024]{2,1,0:T(8,128)} copy-done((f32[4,128,1024]{2,1,0:T(8,128)}, f32[4,128,1024]{2,1,0:T(8,128)S(1)}, u32[]{:S(2)}) %copy-start.2) | copy-done | bytes 2097176
  95.9 5.7 %all-to-all-done.2 = bf16[4,128,640]{2,1,0:T(8,128)(2,1)S(1)} async-done(((bf16[4,128,640]{2,1,0:T(8,128)(2,1)}), bf16[4,128,640]{2,1,0:T(8,128)(2,1)S(1)}, u32[]{:S(2)}, u32[]{:S(2)}) %all-to-all-start.2) | async-done | bytes 655392 | tf_op jit(solution)/shard_map/all_to_all | solution.py:30
  101.6 2.3 %collective-permute-start.6 = (bf16[64,4096]{1,0:T(8,128)(2,1)S(1)}, bf16[64,4096]{1,0:T(8,128)(2,1)}, u32[]{:S(2)}, u32[]{:S(2)}) collective-permute-start(bf16[64,4096]{1,0:T(8,128)(2,1)S(1)} %pad_maximum_fusion.1), channel_id=1, source_target_pairs={{0,16},{8,24},{16,0},{24,8},{1,17},{9,25},{17,1},{25,9},{2,18},{10... | collective-permute-start | bytes 1572872 | tf_op jit(solution)/shard_map/ppermute | solution.py:239
  104.7 0.8 broadcast_in_dim.37
  105.5 6.4 %all-to-all-start.3 = ((bf16[8,8,4096]{2,1,0:T(8,128)(2,1)}), bf16[8,8,4096]{2,1,0:T(8,128)(2,1)S(1)}, u32[]{:S(2)}, u32[]{:S(2)}) async-start(bf16[8,8,4096]{2,1,0:T(8,128)(2,1)} %broadcast_in_dim.37), calls=%async_computation.3 | async-start | bytes 1048576 | tf_op jit(solution)/shard_map/all_to_all | solution.py:30
  112.0 1.6 %copy-done.3 = f32[4,128,1024]{2,1,0:T(8,128)S(1)} copy-done((f32[4,128,1024]{2,1,0:T(8,128)S(1)}, f32[4,128,1024]{2,1,0:T(8,128)}, u32[]{:S(2)}) %copy-start.3) | copy-done | bytes 2097176
  113.6 2.5 %shard_map.116 = bf16[128,512]{1,0:T(8,128)(2,1)} custom-call(s32[1,8]{1,0:T(1,128)S(1)} %copy-done.14, bf16[128,4096]{1,0:T(8,128)(2,1)S(1)} %copy-done, f32[4,128,1024]{2,1,0:T(8,128)S(1)} %copy-done.3, bf16[128,512]{1,0:T(8,128)(2,1)S(1)} %fusion.3.values, bf16[128,4096]{1,0:T(8,128)(2,1)S(1)} %copy-done.1), custom_call_target="tpu_custom_call" | custom-call | flops 268435456 | bytes 5242880 | tf_op jit(solution)/shard_map/pallas_call | solution.py:49
  116.0 1.1 collective-permute-done.6
  117.1 1.1 pad_maximum_fusion
  118.2 3.2 %all-to-all-done.3 = bf16[8,8,4096]{2,1,0:T(8,128)(2,1)S(1)} async-done(((bf16[8,8,4096]{2,1,0:T(8,128)(2,1)}), bf16[8,8,4096]{2,1,0:T(8,128)(2,1)S(1)}, u32[]{:S(2)}, u32[]{:S(2)}) %all-to-all-start.3) | async-done | bytes 524320 | tf_op jit(solution)/shard_map/all_to_all | solution.py:30
  122.1 8.5 %all_to_all.25 = f32[8,8,128]{2,1,0:T(8,128)S(1)} all-to-all(f32[8,8,128]{2,1,0:T(8,128)S(1)} %convolution_bitcast_fusion), channel_id=1, replica_groups=mesh['zh'=2,'x'=4,'c'=2,'y'=4,'zl'=8] {'x','c'}, dimensions={0} | all-to-all | bytes 65536 | tf_op jit(solution)/shard_map/all_to_all | solution.py:30
  (62 shorter events, 7.4 us)
Async XLA Ops:
  0.7 1.0 copy-start.8
  1.7 0.8 copy-start.11
  2.4 0.7 copy-start.12
  3.2 0.7 copy-start.13
  5.3 31.3 %all-to-all-start = ((bf16[8,208,128]{2,1,0:T(8,128)(2,1)}), bf16[8,208,128]{2,1,0:T(8,128)(2,1)S(1)}, u32[]{:S(2)}, u32[]{:S(2)}) async-start(bf16[8,208,128]{2,1,0:T(8,128)(2,1)} %shard_map.113), calls=%async_computation | async-start | bytes 851968 | tf_op jit(solution)/shard_map/all_to_all | solution.py:30
  20.9 15.9 %collective-permute-start = (bf16[128,2048]{1,0:T(8,128)(2,1)}, bf16[128,2048]{1,0:T(8,128)(2,1)S(1)}, u32[]{:S(2)}, u32[]{:S(2)}) collective-permute-start(bf16[128,2048]{1,0:T(8,128)(2,1)} %get-tuple-element.51), channel_id=1, source_target_pairs={{0,8},{8,16},{16,24},{24,0},{1,9},{9,17},{17,25},{25,1},{2,10},{10... | collective-permute-start | bytes 1572872 | tf_op jit(solution)/shard_map/ppermute | solution.py:187
  24.1 14.1 %collective-permute-start.1 = (bf16[128,2048]{1,0:T(8,128)(2,1)S(1)}, bf16[128,2048]{1,0:T(8,128)(2,1)S(1)}, u32[]{:S(2)}, u32[]{:S(2)}) collective-permute-start(bf16[128,2048]{1,0:T(8,128)(2,1)S(1)} %get-tuple-element.50), channel_id=1, source_target_pairs={{0,24},{8,0},{16,8},{24,16},{1,25},{9,1},{17,9},{25,17},{2,26},{10... | collective-permute-start | bytes 1572872 | tf_op jit(solution)/shard_map/ppermute | solution.py:187
  38.1 1.2 copy-start.4
  38.1 38.6 %copy-start.14 = (s32[1,8]{1,0:T(1,128)S(1)}, s32[1,8]{1,0:T(1,128)}, u32[]{:S(2)}) copy-start(s32[1,8]{1,0:T(1,128)} %lengths.3) | copy-start | bytes 100
  39.4 24.2 %all-to-all-start.1 = ((bf16[4,8,144,128]{3,2,1,0:T(8,128)(2,1)}), bf16[4,8,144,128]{3,2,1,0:T(8,128)(2,1)S(1)}, u32[]{:S(2)}, u32[]{:S(2)}) async-start(bf16[4,8,144,128]{3,2,1,0:T(8,128)(2,1)} %broadcast_in_dim.18), calls=%async_computation.1 | async-start | bytes 2359296 | tf_op jit(solution)/shard_map/all_to_all | solution.py:30
  43.4 14.7 %collective-permute-start.2 = (bf16[16,4096]{1,0:T(8,128)(2,1)S(1)}, bf16[16,4096]{1,0:T(8,128)(2,1)S(1)}, u32[]{:S(2)}, u32[]{:S(2)}) collective-permute-start(bf16[16,4096]{1,0:T(8,128)(2,1)S(1)} %bitcast.41), channel_id=1, source_target_pairs={{0,256},{256,0},{1,257},{257,1},{2,258},{258,2},{3,259},{259,3},{4... | collective-permute-start | bytes 393224 | tf_op jit(solution)/shard_map/ppermute | solution.py:239
  51.3 11.4 %collective-permute-start.3 = (bf16[128,2048]{1,0:T(8,128)(2,1)S(1)}, bf16[128,2048]{1,0:T(8,128)(2,1)S(1)}, u32[]{:S(2)}, u32[]{:S(2)}) collective-permute-start(bf16[128,2048]{1,0:T(8,128)(2,1)S(1)} %get-tuple-element.48), channel_id=1, source_target_pairs={{0,16},{8,24},{16,0},{24,8},{1,17},{9,25},{17,1},{25,9},{2,18},{10... | collective-permute-start | bytes 1572872 | tf_op jit(solution)/shard_map/ppermute | solution.py:187
  62.7 0.8 copy-start.6
  63.5 19.5 %collective-permute-start.4 = (bf16[4,8,144,128]{3,2,1,0:T(8,128)(2,1)S(1)}, bf16[4,8,144,128]{3,2,1,0:T(8,128)(2,1)S(1)}, u32[]{:S(2)}, u32[]{:S(2)}) collective-permute-start(bf16[4,8,144,128]{3,2,1,0:T(8,128)(2,1)S(1)} %all-to-all-done.1.own), channel_id=1, source_target_pairs={{0,32},{32,0},{1,33},{33,1},{2,34},{34,2},{3,35},{35,3},{4,36},{36... | collective-permute-start | bytes 3538952 | tf_op jit(solution)/shard_map/ppermute | solution.py:176
  76.9 6.1 %copy-start.5 = (bf16[128,2048]{1,0:T(8,128)(2,1)S(1)}, bf16[128,2048]{1,0:T(8,128)(2,1)}, u32[]{:S(2)}) copy-start(bf16[128,2048]{1,0:T(8,128)(2,1)} %copy-done.4) | copy-start | bytes 1572868
  76.9 6.1 %copy-start.7 = (bf16[128,2048]{1,0:T(8,128)(2,1)S(1)}, bf16[128,2048]{1,0:T(8,128)(2,1)}, u32[]{:S(2)}) copy-start(bf16[128,2048]{1,0:T(8,128)(2,1)} %copy-done.6) | copy-start | bytes 1572868
  79.8 11.3 %collective-permute-start.5 = (bf16[32,4096]{1,0:T(8,128)(2,1)}, bf16[32,4096]{1,0:T(8,128)(2,1)}, u32[]{:S(2)}, u32[]{:S(2)}) collective-permute-start(bf16[32,4096]{1,0:T(8,128)(2,1)} %pad_maximum_fusion.2), channel_id=1, source_target_pairs={{0,8},{8,0},{16,24},{24,16},{1,9},{9,1},{17,25},{25,17},{2,10},{10... | collective-permute-start | bytes 786440 | tf_op jit(solution)/shard_map/ppermute | solution.py:239
  87.1 5.1 %copy-start = (bf16[128,4096]{1,0:T(8,128)(2,1)S(1)}, bf16[128,4096]{1,0:T(8,128)(2,1)}, u32[]{:S(2)}) copy-start(bf16[128,4096]{1,0:T(8,128)(2,1)} %queries.3) | copy-start | bytes 3145732
  87.1 5.1 %copy-start.1 = (bf16[128,4096]{1,0:T(8,128)(2,1)S(1)}, bf16[128,4096]{1,0:T(8,128)(2,1)}, u32[]{:S(2)}) copy-start(bf16[128,4096]{1,0:T(8,128)(2,1)} %upstream.1) | copy-start | bytes 3145732
  87.1 5.1 %copy-start.9 = (bf16[128,512]{1,0:T(8,128)(2,1)S(1)}, bf16[128,512]{1,0:T(8,128)(2,1)}, u32[]{:S(2)}) copy-start(bf16[128,512]{1,0:T(8,128)(2,1)} %keys.1) | copy-start | bytes 393220
  87.1 5.2 %copy-start.10 = (bf16[512,64]{0,1:T(8,128)(2,1)S(1)}, bf16[512,64]{0,1:T(8,128)(2,1)}, u32[]{:S(2)}) copy-start(bf16[512,64]{0,1:T(8,128)(2,1)} %param.14) | copy-start | bytes 196612
  87.1 14.4 %all-to-all-start.2 = ((bf16[4,128,640]{2,1,0:T(8,128)(2,1)}), bf16[4,128,640]{2,1,0:T(8,128)(2,1)S(1)}, u32[]{:S(2)}, u32[]{:S(2)}) async-start(bf16[4,128,640]{2,1,0:T(8,128)(2,1)} %shard_map.114), calls=%async_computation.2 | async-start | bytes 1310720 | tf_op jit(solution)/shard_map/all_to_all | solution.py:30
  94.5 1.3 %copy-start.2 = (f32[4,128,1024]{2,1,0:T(8,128)}, f32[4,128,1024]{2,1,0:T(8,128)S(1)}, u32[]{:S(2)}) copy-start(f32[4,128,1024]{2,1,0:T(8,128)S(1)} %get-tuple-element.43.probs) | copy-start | bytes 6291460
  101.6 2.3 %copy-start.15 = (f32[128,640]{1,0:T(8,128)}, f32[128,640]{1,0:T(8,128)S(1)}, u32[]{:S(2)}) copy-start(f32[128,640]{1,0:T(8,128)S(1)} %convert_reduce_fusion) | copy-start | bytes 983044
  101.6 15.5 %collective-permute-start.6 = (bf16[64,4096]{1,0:T(8,128)(2,1)S(1)}, bf16[64,4096]{1,0:T(8,128)(2,1)}, u32[]{:S(2)}, u32[]{:S(2)}) collective-permute-start(bf16[64,4096]{1,0:T(8,128)(2,1)S(1)} %pad_maximum_fusion.1), channel_id=1, source_target_pairs={{0,16},{8,24},{16,0},{24,8},{1,17},{9,25},{17,1},{25,9},{2,18},{10... | collective-permute-start | bytes 1572872 | tf_op jit(solution)/shard_map/ppermute | solution.py:239
  104.0 7.9 %copy-start.16 = (f32[128,640]{1,0:T(8,128)S(1)}, f32[128,640]{1,0:T(8,128)}, u32[]{:S(2)}) copy-start(f32[128,640]{1,0:T(8,128)} %copy-done.15) | copy-start | bytes 983044
  105.5 15.9 %all-to-all-start.3 = ((bf16[8,8,4096]{2,1,0:T(8,128)(2,1)}), bf16[8,8,4096]{2,1,0:T(8,128)(2,1)S(1)}, u32[]{:S(2)}, u32[]{:S(2)}) async-start(bf16[8,8,4096]{2,1,0:T(8,128)(2,1)} %broadcast_in_dim.37), calls=%async_computation.3 | async-start | bytes 1048576 | tf_op jit(solution)/shard_map/all_to_all | solution.py:30
  112.0 1.6 %copy-start.3 = (f32[4,128,1024]{2,1,0:T(8,128)S(1)}, f32[4,128,1024]{2,1,0:T(8,128)}, u32[]{:S(2)}) copy-start(f32[4,128,1024]{2,1,0:T(8,128)} %copy-done.2) | copy-start | bytes 6291460
  116.0 5.8 %copy-start.17 = (f32[128,128]{1,0:T(8,128)S(1)}, f32[128,128]{1,0:T(8,128)}, u32[]{:S(2)}) copy-start(f32[128,128]{1,0:T(8,128)} %fusion.9) | copy-start | bytes 196612

commit v4 on v3

--- a/solution.py
+++ b/solution.py
@@ -26,8 +26,13 @@
     return math.prod(lax.axis_size(a) for a in axes)
 
 
-def exchange(blocks, axes):
-    return lax.all_to_all(blocks, axes, 0, 0, tiled=False)
+def exchange(blocks, axes, groups=None):
+    return lax.all_to_all(blocks, axes, 0, 0, axis_index_groups=groups, tiled=False)
+
+
+def z_groups():
+    zhs, zs = lax.axis_size("zh"), lax.axis_size("zl")
+    return [[(h ^ (zl & 1)) * zs + zl for zl in range(zs)] for h in range(zhs)]
 
 
 def spread(block, axes):
@@ -167,7 +172,7 @@
         (pltpu.VMEM((RANK, LANES), jnp.float32),),
         moved=1 << 20,
     )(place, norm_gain.reshape(-1, LANES), value_weight, input_basis.T, query_grads)
-    came = exchange(sent, ("zl",))
+    came = exchange(sent, ("zh", "zl"), z_groups())
     queries = came[:, columns:].reshape(zs, length // LANES, rows, LANES)
     return came[:, :columns], queries.transpose(0, 2, 1, 3).reshape(zs * rows, length)
 
@@ -245,7 +250,7 @@
 
 
 def query_steps():
-    return [("zh", b) for b in bits("zh")] + [("y", b) for b in bits("y")]
+    return [("zl", 1)] + [("y", b) for b in bits("y")]
 
 
 def query_order(rows):
@@ -257,11 +262,11 @@
         where[axis] = left % size
         left = left // size
     k, weight = where["zl"] * rows + row, rows * sizes[2]
-    for axis in ("y", "zh"):
-        where[axis] = where[axis] ^ lax.axis_index(axis).astype(jnp.int32)
-    for axis, bit in query_steps():
-        k = k + jnp.where((where[axis] & bit) != 0, weight, 0)
-        weight = weight * 2
+    group = where["zh"] ^ (where["zl"] & 1)
+    own = lax.axis_index("zh") ^ (lax.axis_index("zl") & 1)
+    k = k + (group ^ own.astype(jnp.int32)) * weight
+    distance = where["y"] ^ lax.axis_index("y").astype(jnp.int32)
+    k = k + distance * (weight * sizes[0])
     return (n[:, None] == k[None, :]).astype(jnp.float32)
 
 
@@ -302,14 +307,14 @@
     weights = spread(along_z, ("x",))
     for step in itertools.islice(steps, 1):
         gathered = pair(gathered, *step)
+    weights, gathered, *blocks = lax.optimization_barrier((weights, gathered, *blocks))
+
+    sent = project(blocks, weights)
+    sent, rotated_queries, upstream_grad, tokens = lax.optimization_barrier(
+        (sent, rotated_queries, upstream_grad, tokens)
+    )
     activ = tokens.astype(jnp.float32)
     row_scale = lax.rsqrt(jnp.mean(activ * activ, axis=1, keepdims=True) + epsilon)
-    weights, gathered, *blocks = lax.optimization_barrier((weights, gathered, *blocks))
-
-    sent = project(blocks, weights)
-    sent, rotated_queries, upstream_grad = lax.optimization_barrier(
-        (sent, rotated_queries, upstream_grad)
-    )
     came = exchange(sent, ("y",))
     probs, right = attend_probs(
         rotated_queries, rotated_keys, upstream_grad, example_lengths, output_basis

time: 132 us -> 127 us (0.962)
  starting transfers between devices: 65.1 us -> 53.7 us
  waiting for transfers between devices: 26.6 us -> 32.1 us
  local copies, waits for them, and re-layouts: 12.7 us -> 14.7 us
  other arithmetic: 6.34 us -> 4.89 us
    ppermute x1, starting transfers between devices: 13.1 us -> 5.53 us  [swapped(): return lax.ppermute(block, 'c', [(0, 1), (1, 0)])]
    ppermute x3, starting transfers between devices: 13.4 us -> 7.38 us  [pair(): other = lax.ppermute(block, axis, [(i, i ^ bit) for i in range(size)])]
    all_to_all x4, waiting for transfers between devices: 18 us -> 22.2 us  [exchange(): lax.all_to_all(blocks, axes, 0, 0, axis_index_groups=groups, tiled=False)]
    ppermute x3, waiting for transfers between devices: 5.27 us -> 8.53 us  [share_tokens(): block = lax.ppermute(block, 'y', [(i, (i + s) % ys) for i in range(ys)])]
    unnamed x37 -> x39, local copies, waits for them, and re-layouts: 6.95 us -> 9.05 us
    ppermute x3, waiting for transfers between devices: 3.32 us -> 1.3 us  [pair(): other = lax.ppermute(block, axis, [(i, i ^ bit) for i in range(size)])]
    all_to_all x4, starting transfers between devices: 27.5 us -> 29.4 us  [exchange(): lax.all_to_all(blocks, axes, 0, 0, axis_index_groups=groups, tiled=False)]
    reduce_sum x1, other arithmetic: 2.08 us -> 0.49 us  [on_device(): jnp.mean(activ * activ, axis=1, keepdims=True) + epsilon]
  transfers between devices with their start and end apart: 11 -> 11, of which waited for: 7 -> 5; matrix products, arithmetic and copies ran while one was open for 8% -> 7% of each run, Pallas kernels for 7% -> 7%
where the time goes in v4:
time: 127 us; the launch traced here: 126 us
  starting transfers between devices  53.7 us (42%)
  waiting for transfers between devices  32.1 us (25%)
  local copies, waits for them, and re-layouts  14.7 us (12%)
  Pallas kernels  10.2 us (8%)
  blocking collectives  8.47 us (7%)
  other arithmetic  4.89 us (4%)
    all_to_all x4, starting transfers between devices, exchange(): lax.all_to_all(blocks, axes, 0, 0, axis_index_groups=groups, tiled=False)  29.4 us
    all_to_all x4, waiting for transfers between devices, exchange(): lax.all_to_all(blocks, axes, 0, 0, axis_index_groups=groups, tiled=False)  22.2 us
    ppermute x3, starting transfers between devices, share_tokens(): block = lax.ppermute(block, 'y', [(i, (i + s) % ys) for i in range(ys)])  11.4 us
    pallas_call x4, Pallas kernels, call(): pl.pallas_call(body, out_shape=out_shape, in_specs=[spec(pltpu.SMEM)] + [...  10.2 us
    unnamed x39, local copies, waits for them, and re-layouts  9.05 us
    ppermute x3, waiting for transfers between devices, share_tokens(): block = lax.ppermute(block, 'y', [(i, (i + s) % ys) for i in range(ys)])  8.53 us
    all_to_all x1, blocking collectives, exchange(): lax.all_to_all(blocks, axes, 0, 0, axis_index_groups=groups, tiled=False)  8.47 us
    ppermute x3, starting transfers between devices, pair(): other = lax.ppermute(block, axis, [(i, i ^ bit) for i in range(size)])  7.38 us
  transfers between devices with their start and end apart: 11, of which 5 were waited for; matrix products, arithmetic and copies ran while one was open for 7% of the time, Pallas kernels for 7%

profile of v4, /device:TPU:1, one launch (start us, length us, event | category | flops | bytes accessed | tf_op | source)
XLA Modules:
  0.0 126.1 jit_solution(8129760795225115287)
XLA Ops:
  0.7 0.9 copy-done.8
  3.9 1.4 %shard_map.113 = bf16[8,208,128]{2,1,0:T(8,128)(2,1)} custom-call(s32[3]{0:T(128)S(1)} %pad_add_fusion.1.place, bf16[64,128]{1,0:T(8,128)(2,1)S(1)} %bitcast.37, bf16[256,512]{1,0:T(8,128)(2,1)S(1)} %copy-done.8, bf16[64,256]{1,0:T(8,128)(2,1)S(1)} %bitcast.36, bf16[2,4096]{1,0:T(2,128)(2,1)S(1)} %copy-done.13), custom_call_target="tpu_custom_call" | custom-call | bytes 1048576 | tf_op jit(solution)/shard_map/pallas_call | solution.py:54
  5.3 15.2 %all-to-all-start = ((bf16[8,208,128]{2,1,0:T(8,128)(2,1)}), bf16[8,208,128]{2,1,0:T(8,128)(2,1)S(1)}, u32[]{:S(2)}, u32[]{:S(2)}) async-start(bf16[8,208,128]{2,1,0:T(8,128)(2,1)} %shard_map.113), calls=%async_computation | async-start | bytes 851968 | tf_op jit(solution)/shard_map/all_to_all | solution.py:30
  20.5 2.5 %constant_dynamic-slice_fusion = (bf16[128,2048]{1,0:T(8,128)(2,1)S(1)}, bf16[128,2048]{1,0:T(8,128)(2,1)S(1)}, bf16[128,2048]{1,0:T(8,128)(2,1)S(1)}, bf16[128,2048]{1,0:T(8,128)(2,1)}) fusion(bf16[128,8192]{1,0:T(8,128)(2,1)} %param.10, s32[]{:T(128)S(6)} %select_n.81, s32[]{:T(128)S(6)} %select_n.80, s32[]{:T(128)S(6)} %select_n.79, s32[]{:T(128)S(6)} %select_n.78), kind=kLoop, calls=%fused_computation.44 | loop fusion | bytes 4194320 | tf_op jit(solution)/shard_map/dynamic_slice | solution.py:190
  23.0 3.2 %collective-permute-start = (bf16[128,2048]{1,0:T(8,128)(2,1)}, bf16[128,2048]{1,0:T(8,128)(2,1)S(1)}, u32[]{:S(2)}, u32[]{:S(2)}) collective-permute-start(bf16[128,2048]{1,0:T(8,128)(2,1)} %get-tuple-element.53), channel_id=1, source_target_pairs={{0,8},{8,16},{16,24},{24,0},{1,9},{9,17},{17,25},{25,1},{2,10},{10... | collective-permute-start | bytes 1572872 | tf_op jit(solution)/shard_map/ppermute | solution.py:192
  26.2 3.4 %collective-permute-start.1 = (bf16[128,2048]{1,0:T(8,128)(2,1)S(1)}, bf16[128,2048]{1,0:T(8,128)(2,1)S(1)}, u32[]{:S(2)}, u32[]{:S(2)}) collective-permute-start(bf16[128,2048]{1,0:T(8,128)(2,1)S(1)} %get-tuple-element.52), channel_id=1, source_target_pairs={{0,24},{8,0},{16,8},{24,16},{1,25},{9,1},{17,9},{25,17},{2,26},{10... | collective-permute-start | bytes 1572872 | tf_op jit(solution)/shard_map/ppermute | solution.py:192
  29.5 14.3 %all-to-all-done = bf16[8,208,128]{2,1,0:T(8,128)(2,1)S(1)} async-done(((bf16[8,208,128]{2,1,0:T(8,128)(2,1)}), bf16[8,208,128]{2,1,0:T(8,128)(2,1)S(1)}, u32[]{:S(2)}, u32[]{:S(2)}) %all-to-all-start) | async-done | bytes 426016 | tf_op jit(solution)/shard_map/all_to_all | solution.py:30
  44.0 1.2 broadcast_in_dim.4
  45.2 4.0 %all-to-all-start.1 = ((bf16[4,8,144,128]{3,2,1,0:T(8,128)(2,1)}), bf16[4,8,144,128]{3,2,1,0:T(8,128)(2,1)S(1)}, u32[]{:S(2)}, u32[]{:S(2)}) async-start(bf16[4,8,144,128]{3,2,1,0:T(8,128)(2,1)} %broadcast_in_dim.4), calls=%async_computation.1 | async-start | bytes 2359296 | tf_op jit(solution)/shard_map/all_to_all | solution.py:30
  49.2 1.9 %collective-permute-start.2 = (bf16[16,4096]{1,0:T(8,128)(2,1)S(1)}, bf16[16,4096]{1,0:T(8,128)(2,1)S(1)}, u32[]{:S(2)}, u32[]{:S(2)}) collective-permute-start(bf16[16,4096]{1,0:T(8,128)(2,1)S(1)} %bitcast.41), channel_id=1, source_target_pairs={{0,1},{1,0},{2,3},{3,2},{4,5},{5,4},{6,7},{7,6},{8,9},{9,8},{10,11... | collective-permute-start | bytes 393224 | tf_op jit(solution)/shard_map/ppermute | solution.py:244
  51.1 4.8 %collective-permute-start.3 = (bf16[128,2048]{1,0:T(8,128)(2,1)S(1)}, bf16[128,2048]{1,0:T(8,128)(2,1)S(1)}, u32[]{:S(2)}, u32[]{:S(2)}) collective-permute-start(bf16[128,2048]{1,0:T(8,128)(2,1)S(1)} %get-tuple-element.50), channel_id=1, source_target_pairs={{0,16},{8,24},{16,0},{24,8},{1,17},{9,25},{17,1},{25,9},{2,18},{10... | collective-permute-start | bytes 1572872 | tf_op jit(solution)/shard_map/ppermute | solution.py:192
  56.7 8.5 %collective-permute-done.3.refs_2_ = bf16[128,2048]{1,0:T(8,128)(2,1)S(1)} collective-permute-done((bf16[128,2048]{1,0:T(8,128)(2,1)S(1)}, bf16[128,2048]{1,0:T(8,128)(2,1)S(1)}, u32[]{:S(2)}, u32[]{:S(2)}) %collective-permute-start.3) | collective-permute-done | bytes 524320 | tf_op jit(solution)/shard_map/ppermute | solution.py:192
  65.2 0.8 copy-done.6
  66.0 5.5 %collective-permute-start.4 = (bf16[4,8,144,128]{3,2,1,0:T(8,128)(2,1)S(1)}, bf16[4,8,144,128]{3,2,1,0:T(8,128)(2,1)S(1)}, u32[]{:S(2)}, u32[]{:S(2)}) collective-permute-start(bf16[4,8,144,128]{3,2,1,0:T(8,128)(2,1)S(1)} %all-to-all-done.1.own), channel_id=1, source_target_pairs={{0,32},{32,0},{1,33},{33,1},{2,34},{34,2},{3,35},{35,3},{4,36},{36... | collective-permute-start | bytes 3538952 | tf_op jit(solution)/shard_map/ppermute | solution.py:181
  72.5 3.2 %collective-permute-start.5 = (bf16[32,4096]{1,0:T(8,128)(2,1)}, bf16[32,4096]{1,0:T(8,128)(2,1)}, u32[]{:S(2)}, u32[]{:S(2)}) collective-permute-start(bf16[32,4096]{1,0:T(8,128)(2,1)} %pad_maximum_fusion.2), channel_id=1, source_target_pairs={{0,8},{8,0},{16,24},{24,16},{1,9},{9,1},{17,25},{25,17},{2,10},{10... | collective-permute-start | bytes 786440 | tf_op jit(solution)/shard_map/ppermute | solution.py:244
  75.8 1.0 copy-done.5
  76.9 1.0 copy-done.7
  77.9 4.0 %shard_map.114 = bf16[4,128,640]{2,1,0:T(8,128)(2,1)} custom-call(s32[2]{0:T(128)S(1)} %pad_add_fusion.place, bf16[4,8,144,128]{3,2,1,0:T(8,128)(2,1)S(1)} %all-to-all-done.1.own, bf16[4,8,144,128]{3,2,1,0:T(8,128)(2,1)S(1)} %collective-permute-done.4.partners, bf16[128,2048]{1,0:T(8,128)(2,1)S(1)} %get-tuple-element.31.refs_0_, ...), custom_call_target="tpu_custom_call" | custom-call | flops 1207959552 | bytes 6291456 | tf_op jit(solution)/shard_map/pallas_call | solution.py:54
  81.9 4.0 %all-to-all-start.2 = ((bf16[4,128,640]{2,1,0:T(8,128)(2,1)}), bf16[4,128,640]{2,1,0:T(8,128)(2,1)S(1)}, u32[]{:S(2)}, u32[]{:S(2)}) async-start(bf16[4,128,640]{2,1,0:T(8,128)(2,1)} %shard_map.114), calls=%async_computation.2 | async-start | bytes 1310720 | tf_op jit(solution)/shard_map/all_to_all | solution.py:30
  86.0 1.2 pad_maximum_fusion.1
  87.2 2.3 %shard_map.115 = (f32[4,128,1024]{2,1,0:T(8,128)S(1)}, f32[128,64]{1,0:T(8,128)S(1)}) custom-call(s32[1,8]{1,0:T(1,128)S(1)} %copy-done.14, bf16[128,4096]{1,0:T(8,128)(2,1)S(1)} %copy-done, bf16[128,512]{1,0:T(8,128)(2,1)S(1)} %copy-done.9, bf16[128,4096]{1,0:T(8,128)(2,1)S(1)} %copy-done.1, bf16[64,512]{1,0:T(8,128)(2,1)S(1)} %bitcast.35), custom_call_target="tpu_custom_call" | custom-call | flops 268435456 | bytes 5242880 | tf_op jit(solution)/shard_map/pallas_call | solution.py:54
  89.5 1.3 %copy-done.2 = f32[4,128,1024]{2,1,0:T(8,128)} copy-done((f32[4,128,1024]{2,1,0:T(8,128)}, f32[4,128,1024]{2,1,0:T(8,128)S(1)}, u32[]{:S(2)}) %copy-start.2) | copy-done | bytes 2097176
  91.4 5.0 %all-to-all-done.2 = bf16[4,128,640]{2,1,0:T(8,128)(2,1)S(1)} async-done(((bf16[4,128,640]{2,1,0:T(8,128)(2,1)}), bf16[4,128,640]{2,1,0:T(8,128)(2,1)S(1)}, u32[]{:S(2)}, u32[]{:S(2)}) %all-to-all-start.2) | async-done | bytes 655392 | tf_op jit(solution)/shard_map/all_to_all | solution.py:30
  96.5 2.3 %collective-permute-start.6 = (bf16[64,4096]{1,0:T(8,128)(2,1)S(1)}, bf16[64,4096]{1,0:T(8,128)(2,1)}, u32[]{:S(2)}, u32[]{:S(2)}) collective-permute-start(bf16[64,4096]{1,0:T(8,128)(2,1)S(1)} %pad_maximum_fusion.1), channel_id=1, source_target_pairs={{0,16},{8,24},{16,0},{24,8},{1,17},{9,25},{17,1},{25,9},{2,18},{10... | collective-permute-start | bytes 1572872 | tf_op jit(solution)/shard_map/ppermute | solution.py:244
  99.5 0.8 broadcast_in_dim.5
  100.4 6.1 %all-to-all-start.3 = ((bf16[8,8,4096]{2,1,0:T(8,128)(2,1)}), bf16[8,8,4096]{2,1,0:T(8,128)(2,1)S(1)}, u32[]{:S(2)}, u32[]{:S(2)}) async-start(bf16[8,8,4096]{2,1,0:T(8,128)(2,1)} %broadcast_in_dim.5), calls=%async_computation.3 | async-start | bytes 1048576 | tf_op jit(solution)/shard_map/all_to_all | solution.py:30
  106.6 1.6 %copy-done.3 = f32[4,128,1024]{2,1,0:T(8,128)S(1)} copy-done((f32[4,128,1024]{2,1,0:T(8,128)S(1)}, f32[4,128,1024]{2,1,0:T(8,128)}, u32[]{:S(2)}) %copy-start.3) | copy-done | bytes 2097176
  108.2 2.5 %shard_map.116 = bf16[128,512]{1,0:T(8,128)(2,1)} custom-call(s32[1,8]{1,0:T(1,128)S(1)} %copy-done.14, bf16[128,4096]{1,0:T(8,128)(2,1)S(1)} %copy-done, f32[4,128,1024]{2,1,0:T(8,128)S(1)} %copy-done.3, bf16[128,512]{1,0:T(8,128)(2,1)S(1)} %fusion.3.values, bf16[128,4096]{1,0:T(8,128)(2,1)S(1)} %copy-done.1), custom_call_target="tpu_custom_call" | custom-call | flops 268435456 | bytes 5242880 | tf_op jit(solution)/shard_map/pallas_call | solution.py:54
  110.7 1.3 %collective-permute-done.6 = bf16[64,4096]{1,0:T(8,128)(2,1)} collective-permute-done((bf16[64,4096]{1,0:T(8,128)(2,1)S(1)}, bf16[64,4096]{1,0:T(8,128)(2,1)}, u32[]{:S(2)}, u32[]{:S(2)}) %collective-permute-start.6) | collective-permute-done | bytes 524320 | tf_op jit(solution)/shard_map/ppermute | solution.py:244
  112.0 1.1 pad_maximum_fusion
  113.1 2.9 %all-to-all-done.3 = bf16[8,8,4096]{2,1,0:T(8,128)(2,1)S(1)} async-done(((bf16[8,8,4096]{2,1,0:T(8,128)(2,1)}), bf16[8,8,4096]{2,1,0:T(8,128)(2,1)S(1)}, u32[]{:S(2)}, u32[]{:S(2)}) %all-to-all-start.3) | async-done | bytes 524320 | tf_op jit(solution)/shard_map/all_to_all | solution.py:30
  116.7 8.5 %all_to_all.25 = f32[8,8,128]{2,1,0:T(8,128)S(1)} all-to-all(f32[8,8,128]{2,1,0:T(8,128)S(1)} %convolution_bitcast_fusion), channel_id=1, replica_groups=mesh['zh'=2,'x'=4,'c'=2,'y'=4,'zl'=8] {'x','c'}, dimensions={0} | all-to-all | bytes 65536 | tf_op jit(solution)/shard_map/all_to_all | solution.py:30
  (64 shorter events, 7.1 us)
Async XLA Ops:
  0.7 1.0 copy-start.8
  1.7 0.8 copy-start.11
  2.4 0.7 copy-start.12
  3.1 0.7 copy-start.13
  5.3 38.5 %all-to-all-start = ((bf16[8,208,128]{2,1,0:T(8,128)(2,1)}), bf16[8,208,128]{2,1,0:T(8,128)(2,1)S(1)}, u32[]{:S(2)}, u32[]{:S(2)}) async-start(bf16[8,208,128]{2,1,0:T(8,128)(2,1)} %shard_map.113), calls=%async_computation | async-start | bytes 851968 | tf_op jit(solution)/shard_map/all_to_all | solution.py:30
  23.0 21.0 %collective-permute-start = (bf16[128,2048]{1,0:T(8,128)(2,1)}, bf16[128,2048]{1,0:T(8,128)(2,1)S(1)}, u32[]{:S(2)}, u32[]{:S(2)}) collective-permute-start(bf16[128,2048]{1,0:T(8,128)(2,1)} %get-tuple-element.53), channel_id=1, source_target_pairs={{0,8},{8,16},{16,24},{24,0},{1,9},{9,17},{17,25},{25,1},{2,10},{10... | collective-permute-start | bytes 1572872 | tf_op jit(solution)/shard_map/ppermute | solution.py:192
  26.2 17.8 %collective-permute-start.1 = (bf16[128,2048]{1,0:T(8,128)(2,1)S(1)}, bf16[128,2048]{1,0:T(8,128)(2,1)S(1)}, u32[]{:S(2)}, u32[]{:S(2)}) collective-permute-start(bf16[128,2048]{1,0:T(8,128)(2,1)S(1)} %get-tuple-element.52), channel_id=1, source_target_pairs={{0,24},{8,0},{16,8},{24,16},{1,25},{9,1},{17,9},{25,17},{2,26},{10... | collective-permute-start | bytes 1572872 | tf_op jit(solution)/shard_map/ppermute | solution.py:192
  44.0 1.2 copy-start.4
  44.0 27.6 %copy-start.14 = (s32[1,8]{1,0:T(1,128)S(1)}, s32[1,8]{1,0:T(1,128)}, u32[]{:S(2)}) copy-start(s32[1,8]{1,0:T(1,128)} %lengths.3) | copy-start | bytes 100
  45.2 20.8 %all-to-all-start.1 = ((bf16[4,8,144,128]{3,2,1,0:T(8,128)(2,1)}), bf16[4,8,144,128]{3,2,1,0:T(8,128)(2,1)S(1)}, u32[]{:S(2)}, u32[]{:S(2)}) async-start(bf16[4,8,144,128]{3,2,1,0:T(8,128)(2,1)} %broadcast_in_dim.4), calls=%async_computation.1 | async-start | bytes 2359296 | tf_op jit(solution)/shard_map/all_to_all | solution.py:30
  49.2 6.7 %collective-permute-start.2 = (bf16[16,4096]{1,0:T(8,128)(2,1)S(1)}, bf16[16,4096]{1,0:T(8,128)(2,1)S(1)}, u32[]{:S(2)}, u32[]{:S(2)}) collective-permute-start(bf16[16,4096]{1,0:T(8,128)(2,1)S(1)} %bitcast.41), channel_id=1, source_target_pairs={{0,1},{1,0},{2,3},{3,2},{4,5},{5,4},{6,7},{7,6},{8,9},{9,8},{10,11... | collective-permute-start | bytes 393224 | tf_op jit(solution)/shard_map/ppermute | solution.py:244
  51.1 14.1 %collective-permute-start.3 = (bf16[128,2048]{1,0:T(8,128)(2,1)S(1)}, bf16[128,2048]{1,0:T(8,128)(2,1)S(1)}, u32[]{:S(2)}, u32[]{:S(2)}) collective-permute-start(bf16[128,2048]{1,0:T(8,128)(2,1)S(1)} %get-tuple-element.50), channel_id=1, source_target_pairs={{0,16},{8,24},{16,0},{24,8},{1,17},{9,25},{17,1},{25,9},{2,18},{10... | collective-permute-start | bytes 1572872 | tf_op jit(solution)/shard_map/ppermute | solution.py:192
  65.2 0.8 copy-start.6
  66.0 9.8 %collective-permute-start.4 = (bf16[4,8,144,128]{3,2,1,0:T(8,128)(2,1)S(1)}, bf16[4,8,144,128]{3,2,1,0:T(8,128)(2,1)S(1)}, u32[]{:S(2)}, u32[]{:S(2)}) collective-permute-start(bf16[4,8,144,128]{3,2,1,0:T(8,128)(2,1)S(1)} %all-to-all-done.1.own), channel_id=1, source_target_pairs={{0,32},{32,0},{1,33},{33,1},{2,34},{34,2},{3,35},{35,3},{4,36},{36... | collective-permute-start | bytes 3538952 | tf_op jit(solution)/shard_map/ppermute | solution.py:181
  72.5 13.4 %collective-permute-start.5 = (bf16[32,4096]{1,0:T(8,128)(2,1)}, bf16[32,4096]{1,0:T(8,128)(2,1)}, u32[]{:S(2)}, u32[]{:S(2)}) collective-permute-start(bf16[32,4096]{1,0:T(8,128)(2,1)} %pad_maximum_fusion.2), channel_id=1, source_target_pairs={{0,8},{8,0},{16,24},{24,16},{1,9},{9,1},{17,25},{25,17},{2,10},{10... | collective-permute-start | bytes 786440 | tf_op jit(solution)/shard_map/ppermute | solution.py:244
  75.8 1.0 copy-start.5
  76.9 1.0 copy-start.7
  81.9 5.3 %copy-start = (bf16[128,4096]{1,0:T(8,128)(2,1)S(1)}, bf16[128,4096]{1,0:T(8,128)(2,1)}, u32[]{:S(2)}) copy-start(bf16[128,4096]{1,0:T(8,128)(2,1)} %queries.3) | copy-start | bytes 3145732
  81.9 5.3 %copy-start.1 = (bf16[128,4096]{1,0:T(8,128)(2,1)S(1)}, bf16[128,4096]{1,0:T(8,128)(2,1)}, u32[]{:S(2)}) copy-start(bf16[128,4096]{1,0:T(8,128)(2,1)} %upstream.1) | copy-start | bytes 3145732
  81.9 5.3 %copy-start.9 = (bf16[128,512]{1,0:T(8,128)(2,1)S(1)}, bf16[128,512]{1,0:T(8,128)(2,1)}, u32[]{:S(2)}) copy-start(bf16[128,512]{1,0:T(8,128)(2,1)} %keys.1) | copy-start | bytes 393220
  81.9 5.3 %copy-start.10 = (bf16[512,64]{0,1:T(8,128)(2,1)S(1)}, bf16[512,64]{0,1:T(8,128)(2,1)}, u32[]{:S(2)}) copy-start(bf16[512,64]{0,1:T(8,128)(2,1)} %param.14) | copy-start | bytes 196612
  81.9 14.4 %all-to-all-start.2 = ((bf16[4,128,640]{2,1,0:T(8,128)(2,1)}), bf16[4,128,640]{2,1,0:T(8,128)(2,1)S(1)}, u32[]{:S(2)}, u32[]{:S(2)}) async-start(bf16[4,128,640]{2,1,0:T(8,128)(2,1)} %shard_map.114), calls=%async_computation.2 | async-start | bytes 1310720 | tf_op jit(solution)/shard_map/all_to_all | solution.py:30
  86.0 4.9 %copy-start.15 = (bf16[128,8192]{1,0:T(8,128)(2,1)S(1)}, bf16[128,8192]{1,0:T(8,128)(2,1)}, u32[]{:S(2)}) copy-start(bf16[128,8192]{1,0:T(8,128)(2,1)} %param.10) | copy-start | bytes 6291460
  89.5 1.4 %copy-start.2 = (f32[4,128,1024]{2,1,0:T(8,128)}, f32[4,128,1024]{2,1,0:T(8,128)S(1)}, u32[]{:S(2)}) copy-start(f32[4,128,1024]{2,1,0:T(8,128)S(1)} %get-tuple-element.45.probs) | copy-start | bytes 6291460
  96.5 2.3 %copy-start.16 = (f32[128,640]{1,0:T(8,128)}, f32[128,640]{1,0:T(8,128)S(1)}, u32[]{:S(2)}) copy-start(f32[128,640]{1,0:T(8,128)S(1)} %convert_reduce_fusion) | copy-start | bytes 983044
  96.5 15.5 %collective-permute-start.6 = (bf16[64,4096]{1,0:T(8,128)(2,1)S(1)}, bf16[64,4096]{1,0:T(8,128)(2,1)}, u32[]{:S(2)}, u32[]{:S(2)}) collective-permute-start(bf16[64,4096]{1,0:T(8,128)(2,1)S(1)} %pad_maximum_fusion.1), channel_id=1, source_target_pairs={{0,16},{8,24},{16,0},{24,8},{1,17},{9,25},{17,1},{25,9},{2,18},{10... | collective-permute-start | bytes 1572872 | tf_op jit(solution)/shard_map/ppermute | solution.py:244
  98.9 7.7 %copy-start.17 = (f32[128,640]{1,0:T(8,128)S(1)}, f32[128,640]{1,0:T(8,128)}, u32[]{:S(2)}) copy-start(f32[128,640]{1,0:T(8,128)} %copy-done.16) | copy-start | bytes 983044
  100.4 15.6 %all-to-all-start.3 = ((bf16[8,8,4096]{2,1,0:T(8,128)(2,1)}), bf16[8,8,4096]{2,1,0:T(8,128)(2,1)S(1)}, u32[]{:S(2)}, u32[]{:S(2)}) async-start(bf16[8,8,4096]{2,1,0:T(8,128)(2,1)} %broadcast_in_dim.5), calls=%async_computation.3 | async-start | bytes 1048576 | tf_op jit(solution)/shard_map/all_to_all | solution.py:30
  106.6 1.6 %copy-start.3 = (f32[4,128,1024]{2,1,0:T(8,128)S(1)}, f32[4,128,1024]{2,1,0:T(8,128)}, u32[]{:S(2)}) copy-start(f32[4,128,1024]{2,1,0:T(8,128)} %copy-done.2) | copy-start | bytes 6291460
  110.7 5.8 %copy-start.18 = (f32[128,128]{1,0:T(8,128)S(1)}, f32[128,128]{1,0:T(8,128)}, u32[]{:S(2)}) copy-start(f32[128,128]{1,0:T(8,128)} %fusion.9) | copy-start | bytes 196612
